TPU v7x, 32 devices: a whole 2x2x4 slice. The times are simulated.
32 devices in a mesh: ctx: 16 (over z, y, core), rep: 2 (over x).
Axes of the slice: x: 2, y: 2, z: 4, core: 2. Of those that a mesh axis runs over, the one named last changes fastest.
Arguments:
- tokens: bfloat16 [4096, 8192], P('ctx'), may hold values from -6 to 6
- norm_gain: bfloat16 [8192], replicated, may hold values from 0.099609375 to 1.8984375
- q_weight: bfloat16 [8192, 4096], P('ctx', 'rep'), may hold values from -0.0625 to 0.0625
- q_bias: bfloat16 [4096], P('rep'), may hold values from -48 to 48
- key_value_weight: bfloat16 [8192, 1024], P('ctx', 'rep'), may hold values from -0.0625 to 0.0625
- kv_bias: bfloat16 [1024], P('rep'), may hold values from -8 to 8
- out_weight: bfloat16 [4096, 8192], P('rep', 'ctx'), may hold values from -0.5 to 0.5
Outputs:
- attn_out: bfloat16 [4096, 8192], P(('ctx', 'rep'))
- key_value_cache: bfloat16 [4096, 1024], P('ctx')
All inputs are finite; a program needn't handle non-finite values.
Results may differ from a plain program's by a relative error of at most 0.014.
The roundings to bfloat16 on the way count: a program that leaves them out, or rounds other values in their place, can miss the bound.
Values may be sent and summed in bfloat16 or wider, within the bound.
No kernel may reach another device: no remote copies, remote signals or barrier semaphores. Data moves between devices by JAX's collectives and lax.ppermute only.
A program may use at most 128 MiB of HBM per device.

v0:
```python
import jax
import jax.numpy as jnp
from jax import lax
from jax.sharding import PartitionSpec as P

HEAD_SIZE = 128
QUERY_HEADS = 32
KEY_VALUE_HEADS = 4


rope_base = 1000000.0


def apply_rotation(value_rows, token_positions):
    middle = value_rows.shape[-1] // 2
    exponent = jnp.arange(middle, dtype=jnp.float32) * (2.0 / value_rows.shape[-1])
    inverse = rope_base ** (-exponent)
    angles = token_positions.astype(jnp.float32)[:, None] * inverse[None, :]
    cosine = jnp.cos(angles)[:, None, :]
    sine_part = jnp.sin(angles)[:, None, :]
    leading = value_rows[..., :middle]
    trailing = value_rows[..., middle:]
    return jnp.concatenate(
        [leading * cosine - trailing * sine_part, trailing * cosine + leading * sine_part], axis=-1
    )


def normalize(tokens, norm_gain):
    values_in = tokens.astype(jnp.float32)
    scale_row = lax.rsqrt(jnp.mean(values_in * values_in, axis=-1, keepdims=True) + 1e-06)
    return (values_in * scale_row * norm_gain.astype(jnp.float32)).astype(jnp.bfloat16)


def attend_block(carry, query_rows, query_pos, key_rows, value_rows):
    maximum, total, accum = carry
    scores = jnp.einsum(
        "rgjd,pgd->gjrp", query_rows, key_rows, preferred_element_type=jnp.float32
    ) * query_rows.shape[-1] ** (-0.5)
    key_pos = jnp.arange(key_rows.shape[0], dtype=jnp.int32)
    allowed = key_pos[None, :] <= query_pos[:, None]
    scores = jnp.where(allowed, scores, -1e30)
    fresh = jnp.maximum(maximum, jnp.max(scores, axis=-1))
    expo = jnp.where(allowed, jnp.exp(scores - fresh[..., None]), 0.0)
    total = jnp.sum(expo, axis=-1)
    summed = jnp.einsum(
        "gjrp,pgd->gjrd", expo.astype(jnp.bfloat16), value_rows, preferred_element_type=jnp.float32
    )
    accum = summed
    return (fresh, total, accum)


def guarded(carry, query_rows, query_pos, key_rows, value_rows, start):

    def active(state):
        return attend_block(state, query_rows, query_pos, key_rows, value_rows)

    def passive(state):
        return state

    return lax.cond(start <= jnp.max(query_pos), active, passive, carry)


def empty_state(key_value_heads, inner, count):
    return (
        jnp.full((key_value_heads, inner, count), -1e30, jnp.float32),
        jnp.zeros((key_value_heads, inner, count), jnp.float32),
        jnp.zeros((key_value_heads, inner, count, HEAD_SIZE), jnp.float32),
    )


def finish_state(state, count, local_heads):
    maximum, total, accum = state
    result = accum / total[..., None]
    return (
        jnp.transpose(result, (2, 0, 1, 3))
        .reshape(count, local_heads * HEAD_SIZE)
        .astype(jnp.bfloat16)
    )


def per_device(tokens, norm_gain, q_weight, q_bias, key_value_weight, kv_bias, out_weight):
    rows = tokens.shape[0]
    ctx_index = lax.axis_index("ctx")
    rep_index = lax.axis_index("rep")
    head_group = QUERY_HEADS // KEY_VALUE_HEADS
    local_heads = q_weight.shape[1] // HEAD_SIZE
    key_value_heads = max(1, local_heads // head_group)
    inner = local_heads // key_value_heads
    normed = normalize(tokens, norm_gain)
    pieces = (
        lax.all_gather(q_weight, "ctx", axis=0, tiled=True),
        lax.all_gather(key_value_weight, "ctx", axis=0, tiled=True),
    )
    query_sum = jnp.dot(normed, pieces[0], preferred_element_type=jnp.float32)
    key_value_sum = jnp.dot(normed, pieces[1], preferred_element_type=jnp.float32)
    token_positions = ctx_index * rows + jnp.arange(rows, dtype=jnp.int32)
    query_rows = apply_rotation(
        (query_sum + q_bias.astype(jnp.float32)).reshape(rows, local_heads, HEAD_SIZE),
        token_positions,
    ).astype(jnp.bfloat16)
    blocks = key_value_weight.shape[1] // HEAD_SIZE
    kv_full = (key_value_sum + kv_bias.astype(jnp.float32)).reshape(rows, blocks, HEAD_SIZE)
    block_numbers = rep_index * blocks + jnp.arange(blocks, dtype=jnp.int32)
    key_flag = (block_numbers < KEY_VALUE_HEADS)[None, :, None]
    kv_local = (
        jnp.where(key_flag, apply_rotation(kv_full, token_positions), kv_full)
        .astype(jnp.bfloat16)
        .reshape(rows, blocks * HEAD_SIZE)
    )
    key_value_cache = lax.all_gather(kv_local, "rep", axis=1, tiled=True)
    leading_head = rep_index * local_heads // head_group
    key_rows = lax.dynamic_slice_in_dim(
        key_value_cache, leading_head * HEAD_SIZE, key_value_heads * HEAD_SIZE, 1
    ).reshape(rows, key_value_heads, HEAD_SIZE)
    value_rows = lax.dynamic_slice_in_dim(
        key_value_cache,
        (KEY_VALUE_HEADS + leading_head) * HEAD_SIZE,
        key_value_heads * HEAD_SIZE,
        1,
    ).reshape(rows, key_value_heads, HEAD_SIZE)
    grouped_rows = query_rows.reshape(rows, key_value_heads, inner, HEAD_SIZE)
    middle = rows // 2
    query_sets = (
        (grouped_rows[:middle], token_positions[:middle]),
        (grouped_rows[middle:], token_positions[middle:]),
    )
    start_states = tuple(
        (empty_state(key_value_heads, inner, qset[0].shape[0]) for qset in query_sets)
    )
    pieces = (
        lax.all_gather(key_rows, "ctx", axis=0, tiled=True),
        lax.all_gather(value_rows, "ctx", axis=0, tiled=True),
    )
    start = jnp.int32(0)
    states = tuple(
        (
            guarded(state, qset[0], qset[1], pieces[0], pieces[1], start)
            for state, qset in zip(start_states, query_sets)
        )
    )
    lower_out = finish_state(states[0], middle, local_heads)
    upper_out = finish_state(states[1], rows - middle, local_heads)
    attended = jnp.concatenate([lower_out, upper_out], axis=0)
    terms = jnp.dot(
        attended,
        lax.all_gather(out_weight, "ctx", axis=1, tiled=True),
        preferred_element_type=jnp.float32,
    )
    summed = lax.psum_scatter(terms.astype(jnp.bfloat16), "rep", scatter_dimension=0, tiled=True)
    return (summed, key_value_cache)


def solution(mesh):
    in_specs = (
        P("ctx", None),
        P(),
        P("ctx", "rep"),
        P("rep"),
        P("ctx", "rep"),
        P("rep"),
        P("rep", "ctx"),
    )
    out_specs = (P(("ctx", "rep"), None), P("ctx", None))
    return jax.shard_map(
        per_device, mesh=mesh, in_specs=in_specs, out_specs=out_specs, check_vma=False
    )
```

profile of v0, /device:TPU:28, one launch (start us, length us, event | category | flops | bytes accessed | tf_op | source)
XLA Modules:
  0.0 587.2 jit_solution(4895024759344148444)
XLA Ops:
  7.2 0.7 all-gather.8.cloned.1.call-update
  7.9 0.0 all-gather.6.cloned.1.call-start
  7.9 0.7 all-gather.6.cloned.1.call-update
  8.6 0.0 all-gather.10.cloned.1.call-start
  8.7 0.7 convert_element_type.63
  9.4 0.7 convert_element_type.67
  10.2 0.1 broadcast_bitcast_fusion
  10.2 3.1 fusion.24
  13.3 0.5 multiply_cosine_fusion
  13.9 69.5 %all-gather.8.cloned.1.call-done = bf16[8192,512]{1,0:T(8,128)(2,1)} async-done(((bf16[512,512]{1,0:T(8,128)(2,1)}), bf16[8192,512]{1,0:T(8,128)(2,1)}) %all-gather.8.cloned.1.call-update) | async-done | bytes 8388624 | tf_op jit(solution)/shard_map/all_gather | solution.py:92
  83.4 7.0 %convolution_add_fusion.1 = f32[256,512]{1,0:T(8,128)S(1)} fusion(bf16[8192,512]{1,0:T(8,128)(2,1)} %all-gather.8.cloned.1.call-done, bf16[256,8192]{1,0:T(8,128)(2,1)} %param.11, f32[8192]{0:T(1024)S(1)} %convert_element_type.63, f32[256]{0:T(256)S(1)} %add_rsqrt_fusion, f32[512]{0:T(512)S(1)} %convert_element_type.67), kind=kOutput, calls=%fused_computation.40 | convolution fusion | flops 2156003328 | bytes 13143040 | tf_op jit(solution)/shard_map/dot_general | solution.py:95
  90.5 0.2 reshape.113
  90.7 0.5 multiply_subtract_fusion
  91.1 0.4 pad_maximum_fusion.1
  91.5 0.1 fusion.33
  91.6 9.2 %all_gather.20 = bf16[256,1024]{1,0:T(8,128)(2,1)S(1)} all-gather(bf16[256,512]{1,0:T(8,128)(2,1)S(1)} %fusion.33), channel_id=1, replica_groups=mesh['ctx'=16,'rep'=2] {'rep'}, dimensions={1}, use_global_device_ids=true | all-gather | bytes 786432 | tf_op jit(solution)/shard_map/all_gather | solution.py:110
  100.8 0.8 copy-done
  101.6 0.8 copy.17
  102.4 0.0 all-gather.12.cloned.1.call-start
  102.4 0.8 copy.18
  103.2 0.0 all-gather.14.cloned.1.call-start
  103.2 0.5 all-gather.14.cloned.1.call-update
  103.8 0.2 reduce-scatter.2.cloned.1.call-start
  104.0 0.7 slice_reduce_fusion.1
  106.0 147.1 %all-gather.6.cloned.1.call-done = bf16[8192,2048]{1,0:T(8,128)(2,1)} async-done(((bf16[512,2048]{1,0:T(8,128)(2,1)}), bf16[8192,2048]{1,0:T(8,128)(2,1)}) %all-gather.6.cloned.1.call-update) | async-done | bytes 33554448 | tf_op jit(solution)/shard_map/all_gather | solution.py:91
  253.1 16.3 %fusion.27 = f32[32,8,16,128]{3,1,2,0:T(8,128)S(1)} fusion(bf16[8192,2048]{1,0:T(8,128)(2,1)} %all-gather.6.cloned.1.call-done, bf16[256,8192]{1,0:T(8,128)(2,1)} %param.11, f32[8192]{0:T(1024)S(1)} %convert_element_type.63, f32[256]{0:T(256)S(1)} %add_rsqrt_fusion, f32[2048]{0:T(1024)S(1)} %convert_element_type.65), kind=kOutput, calls=%fused_computation.39 | convolution fusion | flops 8598847488 | bytes 39887872 | tf_op jit(solution)/shard_map/dot_general | solution.py:94
  269.4 0.4 copy.45
  269.8 0.7 fusion.36
  270.5 1.4 subtract_convert_fusion
  271.8 0.6 pad_maximum_fusion
  272.4 23.5 %all-gather.10.cloned.1.call-done = bf16[4096,2,128]{0,2,1:T(8,128)(2,1)} async-done(((bf16[256,2,128]{0,2,1:T(8,128)(2,1)}), bf16[4096,2,128]{0,2,1:T(8,128)(2,1)}) %all-gather.10.cloned.1.call-update) | async-done | bytes 2097168 | tf_op jit(solution)/shard_map/all_gather | solution.py:131
  295.9 42.2 %all-gather.12.cloned.1.call-done = bf16[4096,2,128]{0,2,1:T(8,128)(2,1)} async-done(((bf16[256,2,128]{0,2,1:T(8,128)(2,1)}), bf16[4096,2,128]{0,2,1:T(8,128)(2,1)}) %all-gather.12.cloned.1.call-update) | async-done | bytes 2097168 | tf_op jit(solution)/shard_map/all_gather | solution.py:132
  338.1 48.1 %conditional.2 = (f32[2,8,128]{2,1,0:T(8,128)S(1)}, f32[2,8,128,128]{2,3,1,0:T(8,128)S(1)}) conditional(s32[]{:T(128)} %convert_element_type.61, () %tuple.24, (s32[128]{0:T(128)S(1)}, bf16[256,16,128]{2,0,1:T(8,128)(2,1)S(1)}, bf16[4096,2,128]{0,2,1:T(8,128)(2,1)}, bf16[4096,2,128]{0,2,1:T(8,128)(2,1)}) %tuple.25), branch_computations={%region_2.3_spmd, %region_3.6_spmd} | conditional | flops 4404541440 | bytes 109625872 | solution.py:60
  338.1 0.3 iota_compare_fusion
  338.5 16.6 %fusion = (f32[2,8,128]{2,1,0:T(8,128)S(1)}, f32[2,4096,128,8]{2,1,3,0:T(8,128)}) fusion(pred[128,4096]{0,1:T(8,128)(4,1)S(1)} %iota_compare_fusion, bf16[128,2,8,128]{3,0,2,1:T(8,128)(2,1)S(1)} %bitcast.74, bf16[4096,2,128]{0,2,1:T(8,128)(2,1)} %get-tuple-element.40), kind=kOutput, calls=%fused_computation.2 | convolution fusion | flops 2172647424 | bytes 36708352 | tf_op jit(solution)/shard_map/cond/branch_1_fun/rgjd,pgd->gjrp/dot_general | solution.py:36
  355.1 15.9 %fusion.3 = f32[2,8,128,128]{2,3,1,0:T(8,128)S(1)} fusion(f32[2,4096,128,8]{2,1,3,0:T(8,128)} %get-tuple-element.51, f32[2,8,128]{2,1,0:T(8,128)S(1)} %broadcast_maximum_fusion, pred[128,4096]{0,1:T(8,128)(4,1)S(1)} %iota_compare_fusion, bf16[4096,2,128]{0,2,1:T(8,128)(2,1)} %get-tuple-element.41), kind=kOutput, calls=%fused_computation.5 | convolution fusion | flops 2189426688 | bytes 37232640 | tf_op jit(solution)/shard_map/cond | solution.py:60
  371.0 15.2 %fusion.2 = f32[2,8,128]{2,1,0:T(8,128)S(1)} fusion(f32[2,4096,128,8]{2,1,3,0:T(8,128)} %get-tuple-element.51, f32[2,8,128]{2,1,0:T(8,128)S(1)} %broadcast_maximum_fusion, pred[128,4096]{0,1:T(8,128)(4,1)S(1)} %iota_compare_fusion), kind=kLoop, calls=%fused_computation.4 | loop fusion | flops 41940992 | bytes 34095104 | tf_op jit(solution)/shard_map/cond/branch_1_fun/reduce_sum | solution.py:44
  386.3 47.8 %conditional.3 = (f32[2,8,128]{2,1,0:T(8,128)S(1)}, f32[2,8,128,128]{2,3,1,0:T(8,128)S(1)}) conditional(s32[]{:T(128)} %convert_element_type.72, () %tuple.26, (s32[128]{0:T(128)S(1)}, bf16[256,16,128]{2,0,1:T(8,128)(2,1)S(1)}, bf16[4096,2,128]{0,2,1:T(8,128)(2,1)}, bf16[4096,2,128]{0,2,1:T(8,128)(2,1)}) %tuple.27), branch_computations={%region_7.8_spmd, %region_8.11_spmd} | conditional | flops 4404541440 | bytes 109625872 | solution.py:60
  386.5 0.3 iota_compare_fusion.1
  386.9 15.7 %fusion.12 = (f32[2,8,128]{2,1,0:T(8,128)S(1)}, f32[2,4096,128,8]{2,1,3,0:T(8,128)}) fusion(pred[128,4096]{0,1:T(8,128)(4,1)S(1)} %iota_compare_fusion.1, bf16[128,2,8,128]{3,0,2,1:T(8,128)(2,1)S(1)} %bitcast.75, bf16[4096,2,128]{0,2,1:T(8,128)(2,1)} %get-tuple-element.44), kind=kOutput, calls=%fused_computation.17 | convolution fusion | flops 2172647424 | bytes 36708352 | tf_op jit(solution)/shard_map/cond/branch_1_fun/rgjd,pgd->gjrp/dot_general | solution.py:36
  402.6 16.1 %fusion.15 = f32[2,8,128,128]{2,3,1,0:T(8,128)S(1)} fusion(f32[2,4096,128,8]{2,1,3,0:T(8,128)} %get-tuple-element.53, f32[2,8,128]{2,1,0:T(8,128)S(1)} %broadcast_maximum_fusion.1, pred[128,4096]{0,1:T(8,128)(4,1)S(1)} %iota_compare_fusion.1, bf16[4096,2,128]{0,2,1:T(8,128)(2,1)} %get-tuple-element.45), kind=kOutput, calls=%fused_computation.20 | convolution fusion | flops 2189426688 | bytes 37232640 | tf_op jit(solution)/shard_map/cond | solution.py:60
  418.7 15.1 %fusion.14 = f32[2,8,128]{2,1,0:T(8,128)S(1)} fusion(f32[2,4096,128,8]{2,1,3,0:T(8,128)} %get-tuple-element.53, f32[2,8,128]{2,1,0:T(8,128)S(1)} %broadcast_maximum_fusion.1, pred[128,4096]{0,1:T(8,128)(4,1)S(1)} %iota_compare_fusion.1), kind=kLoop, calls=%fused_computation.19 | loop fusion | flops 41940992 | bytes 34095104 | tf_op jit(solution)/shard_map/cond/branch_1_fun/reduce_sum | solution.py:44
  434.1 0.1 divide_convert_fusion.1
  434.2 0.1 divide_convert_fusion
  434.3 73.2 %all-gather.14.cloned.1.call-done = bf16[2048,8192]{1,0:T(8,128)(2,1)} async-done(((bf16[2048,512]{1,0:T(8,128)(2,1)}), bf16[2048,8192]{1,0:T(8,128)(2,1)}) %all-gather.14.cloned.1.call-update) | async-done | bytes 33554448 | tf_op jit(solution)/shard_map/all_gather | solution.py:146
  507.6 16.6 %convolution_convert_fusion = bf16[256,8192]{1,0:T(8,128)(2,1)} fusion(bf16[2048,8192]{1,0:T(8,128)(2,1)} %all-gather.14.cloned.1.call-done, bf16[128,2048]{0,1:T(8,128)(2,1)S(1)} %bitcast.73, bf16[128,2048]{0,1:T(8,128)(2,1)S(1)} %bitcast.72), kind=kOutput, calls=%fused_computation.32 | convolution fusion | flops 8594128896 | bytes 38797312 | tf_op jit(solution)/shard_map/dot_general | solution.py:144
  524.2 55.4 %reduce-scatter.2.cloned.1.call-done = bf16[128,8192]{1,0:T(8,128)(2,1)} async-done(((bf16[256,8192]{1,0:T(8,128)(2,1)}), bf16[128,8192]{1,0:T(8,128)(2,1)}) %reduce-scatter.2.cloned.1.call-update) | async-done | bytes 2097168 | tf_op jit(solution)/shard_map/reduce_scatter | solution.py:149
  579.6 0.8 copy.61
  (19 shorter events, 0.2 us)
Async XLA Ops:
  7.2 76.3 %all-gather.8.cloned.1.call-start = ((), (), s32[]{:S(2)}) async-start(), calls=%async_computation.2 | async-start | bytes 8912896 | tf_op jit(solution)/shard_map/all_gather | solution.py:92
  7.9 245.2 %all-gather.6.cloned.1.call-start = ((), (), s32[]{:S(2)}) async-start(), calls=%async_computation.1 | async-start | bytes 35651584 | tf_op jit(solution)/shard_map/all_gather | solution.py:91
  8.6 287.3 %all-gather.10.cloned.1.call-start = ((), (), s32[]{:S(2)}) async-start(), calls=%async_computation.3 | async-start | bytes 2228224 | tf_op jit(solution)/shard_map/all_gather | solution.py:131
  90.5 13.6 %copy-start.2 = (bf16[2048]{0:T(1024)(128)(2,1)S(1)}, bf16[2048]{0:T(1024)(128)(2,1)}, u32[]{:S(2)}) copy-start(bf16[2048]{0:T(1024)(128)(2,1)} %param.14) | copy-start | bytes 12292
  100.8 0.8 copy-start
  102.4 235.7 %all-gather.12.cloned.1.call-start = ((), (), s32[]{:S(2)}) async-start(), calls=%async_computation.4 | async-start | bytes 2228224 | tf_op jit(solution)/shard_map/all_gather | solution.py:132
  103.2 404.4 %all-gather.14.cloned.1.call-start = ((), (), s32[]{:S(2)}) async-start(), calls=%async_computation.5 | async-start | bytes 35651584 | tf_op jit(solution)/shard_map/all_gather | solution.py:146
  103.8 475.8 %reduce-scatter.2.cloned.1.call-start = ((), (), s32[]{:S(2)}) async-start(), calls=%async_computation.6 | async-start | bytes 6291456 | tf_op jit(solution)/shard_map/reduce_scatter | solution.py:149
  507.6 72.0 %copy-start.1 = (bf16[256,1024]{1,0:T(8,128)(2,1)S(1)}, bf16[256,1024]{1,0:T(8,128)(2,1)}, u32[]{:S(2)}) copy-start(bf16[256,1024]{1,0:T(8,128)(2,1)} %copy-done) | copy-start | bytes 1572868
Sparse Core Ops, SparseCore 0:
  10.2 73.2 all-gather.7
  85.0 167.9 all-gather.5
  255.8 40.1 all-gather.9
  298.0 40.1 all-gather.11
  339.5 168.0 all-gather.13
  524.3 55.2 reduce-scatter.1
where the time goes:
time: 590 us; the launch traced here: 587 us
  waiting for transfers between devices  413 us (70%)
  matrix products  104 us (18%)
  other arithmetic  39.9 us (7%)
  between operations  15.5 us (3%)
  blocking collectives  9.15 us (2%)
    all_gather x1, waiting for transfers between devices, per_device(): lax.all_gather(q_weight, 'ctx', axis=0, tiled=True)  147 us
    all_gather x1, waiting for transfers between devices, per_device(): lax.all_gather(out_weight, 'ctx', axis=1, tiled=True)  73.2 us
    all_gather x1, waiting for transfers between devices, per_device(): lax.all_gather(key_value_weight, 'ctx', axis=0, tiled=True)  69.5 us
    reduce_scatter x1, waiting for transfers between devices, per_device(): lax.psum_scatter(terms.astype(jnp.bfloat16), 'rep', scatter_dimension=0,...  55.4 us
    all_gather x1, waiting for transfers between devices, per_device(): lax.all_gather(value_rows, 'ctx', axis=0, tiled=True)  42.2 us
    dot_general x2, matrix products, attend_block(): jnp.einsum('rgjd,pgd->gjrp', query_rows, key_rows, preferred_element_type...  32.2 us
    cond x2, matrix products, guarded(): return lax.cond(start <= jnp.max(query_pos), active, passive, carry)  32 us
    reduce_sum x2, other arithmetic, attend_block(): total = jnp.sum(expo, axis=-1)  30.3 us
  transfers between devices with their start and end apart: 6, of which 6 were waited for; matrix products, arithmetic and copies ran while one was open for 22% of the time, Pallas kernels for 0%

commit v1 on v0

v1 whole, which is shorter than its diff:
```python
import functools

import jax
import jax.numpy as jnp
from jax import lax
from jax.experimental import pallas as pl
from jax.experimental.pallas import tpu as pltpu
from jax.sharding import PartitionSpec as P

HEAD_SIZE = 128
QUERY_HEADS = 32
KEY_VALUE_HEADS = 4
ROPE_BASE = 1000000.0
CORE, Y, SPLIT = 1, 2, 4
VMEM_LIMIT = 48 * 1024 * 1024
LOG2E = 1.4426950408889634
VM = pl.BlockSpec(memory_space=pltpu.VMEM)
SM = pl.BlockSpec(memory_space=pltpu.SMEM)


def swap(x, mask):
    n = lax.axis_size("ctx")
    return lax.ppermute(x, "ctx", [(i, i ^ mask) for i in range(n)])


def swap_rep(x, mask):
    n = lax.axis_size("rep")
    return lax.ppermute(x, "rep", [(i, i ^ mask) for i in range(n)])


def after(x, *tokens):
    tokens = tuple(t for t in tokens if t is not None)
    if not tokens:
        return x
    return lax.optimization_barrier((x,) + tokens)[0]


def gather_rep(x, axis):
    rep = lax.axis_index("rep")
    bit = 1
    while bit < lax.axis_size("rep"):
        other = swap_rep(x, bit)
        high = (rep & bit) != 0
        x = jnp.concatenate([jnp.where(high, other, x), jnp.where(high, x, other)], axis=axis)
        bit *= 2
    return x


def call(body, out_shape, specs, flops, nbytes, args, scratch=(), name=None):
    outs = tuple(out_shape)
    return pl.pallas_call(
        body,
        out_shape=outs,
        in_specs=specs,
        out_specs=tuple(VM for _ in outs),
        scratch_shapes=list(scratch),
        compiler_params=pltpu.CompilerParams(vmem_limit_bytes=VMEM_LIMIT),
        cost_estimate=pl.CostEstimate(flops=flops, bytes_accessed=nbytes, transcendentals=0),
        name=name,
    )(*args)


def norm_body(masks, place, tokens, gain, own, send):
    ctx = place[0]
    rows, width = tokens.shape
    kb = own.shape[1] // len(masks)
    step = 32

    def chunk(i, carry):
        part = pl.ds(i * step, step)
        t = tokens[part, :].astype(jnp.float32)
        scale = lax.rsqrt(jnp.sum(t * t, axis=-1, keepdims=True) * (1.0 / width) + 1e-06)
        for extra, ref in ((0, own), (SPLIT, send)):
            for j, m in enumerate(masks):
                block = pl.ds(pl.multiple_of((ctx ^ (m | extra)) * kb, 128), kb)
                v = tokens[part, block].astype(jnp.float32) * scale * gain[:, block].astype(jnp.float32)
                ref[part, j * kb : (j + 1) * kb] = v.astype(jnp.bfloat16)
        return carry

    lax.fori_loop(0, rows // step, chunk, 0)


def project_body(a_own, a_recv, *refs):
    weights, outs = refs[:-2], refs[-2:]
    kb = weights[0].shape[0]
    for a, out in zip((a_own, a_recv), outs):
        total = None
        for j, w in enumerate(weights):
            part = jnp.dot(a[:, j * kb : (j + 1) * kb], w[...], preferred_element_type=jnp.float32)
            total = part if total is None else total + part
        out[...] = total.astype(out.dtype)


def rotate(v, cosine, sine):
    half = HEAD_SIZE // 2
    turned = jnp.concatenate([v[:, half:], v[:, :half]], axis=1)
    return v * cosine + turned * sine


def attend_body(n_bits, place, mine, other, bias, cosine, sine, keys, values, out, q, acc, top, total):
    ctx = place[0]
    rows, width = mine.shape
    heads = width // HEAD_SIZE
    for h in range(heads):
        cols = slice(h * HEAD_SIZE, (h + 1) * HEAD_SIZE)
        v = mine[:, cols] + other[:, cols].astype(jnp.float32) + bias[:, cols].astype(jnp.float32)
        q[h * rows : (h + 1) * rows, :] = rotate(v, cosine[...], sine[...]).astype(jnp.bfloat16)
    factor = LOG2E * HEAD_SIZE ** (-0.5)

    def scores(pos):
        k = keys[pl.ds(pl.multiple_of(pos * rows, 128), rows), :]
        return lax.dot_general(q[...], k, (((1,), (1,)), ((), ())), preferred_element_type=jnp.float32)

    def weighted(p, pos):
        v = values[pl.ds(pl.multiple_of(pos * rows, 128), rows), :]
        return jnp.dot(p.astype(jnp.bfloat16), v, preferred_element_type=jnp.float32)

    s = scores(0)
    r = lax.broadcasted_iota(jnp.int32, s.shape, 0) % rows
    c = lax.broadcasted_iota(jnp.int32, s.shape, 1)
    s = jnp.where(c <= r, s, -1e30)
    m = jnp.max(s, axis=-1, keepdims=True)
    p = jnp.exp2((s - m) * factor)
    top[...] = m
    total[...] = jnp.sum(p, axis=-1, keepdims=True)
    acc[...] = weighted(p, 0)

    def block(b, carry):
        k = ctx ^ b
        pos = (k >> 2) | ((k & 2) << (n_bits - 3)) | ((k & 1) << (n_bits - 1))
        s = scores(pos)
        old = top[...]
        m = jnp.maximum(old, jnp.max(s, axis=-1, keepdims=True))
        p = jnp.exp2((s - m) * factor)
        shrink = jnp.exp2((old - m) * factor)
        top[...] = m
        total[...] = total[...] * shrink + jnp.sum(p, axis=-1, keepdims=True)
        acc[...] = acc[...] * shrink + weighted(p, pos)
        return carry

    lax.fori_loop(0, ctx, block, 0)
    result = acc[...] / total[...]
    for h in range(heads):
        out[:, h * HEAD_SIZE : (h + 1) * HEAD_SIZE] = result[h * rows : (h + 1) * rows].astype(jnp.bfloat16)


def output_body(n_att, place, *refs):
    own, recv = refs[:n_att], refs[n_att : 2 * n_att]
    weights, outs = refs[2 * n_att : -1], refs[-1]
    rep = place[1]
    rows = own[0].shape[0]
    members = outs.shape[0]
    size = rows // members
    wide = own[0].shape[1]
    n = weights[0].shape[1]
    for far in range(members):
        part = pl.ds(pl.multiple_of((rep ^ far) * size, size), size)
        for i, att in enumerate((own, recv)):
            for j, w in enumerate(weights):
                total = None
                for a, piece in enumerate(att):
                    term = jnp.dot(piece[part, :], w[a * wide : (a + 1) * wide, :], preferred_element_type=jnp.float32)
                    total = term if total is None else total + term
                outs[far, i * size : (i + 1) * size, j * n : (j + 1) * n] = total.astype(jnp.bfloat16)


def place_body(masks, n_sub, place, *refs):
    own, recv, out = refs[:n_sub], refs[n_sub:-1], refs[-1]
    ctx = place[0]
    sub = own[0].shape[1] // len(masks)
    block = sub * n_sub
    for extra, group in ((0, own), (SPLIT, recv)):
        for s, ref in enumerate(group):
            for j, m in enumerate(masks):
                start = (ctx ^ (m | extra)) * block + s * sub
                out[:, pl.ds(pl.multiple_of(start, 128), sub)] = ref[:, j * sub : (j + 1) * sub]


def per_device(tokens, norm_gain, q_weight, q_bias, kv_weight, kv_bias, out_weight):
    rows, width = tokens.shape
    n_ctx, n_rep = lax.axis_size("ctx"), lax.axis_size("rep")
    n_bits = n_ctx.bit_length() - 1
    ctx, rep = lax.axis_index("ctx"), lax.axis_index("rep")
    place = jnp.stack([ctx, rep]).astype(jnp.int32)
    head_group = QUERY_HEADS // KEY_VALUE_HEADS
    local_heads = q_weight.shape[1] // HEAD_SIZE
    kv_heads = max(1, local_heads // head_group)
    high_bits = [1 << b for b in range(3, n_bits)]
    masks = [0]
    for bit in high_bits + [Y, CORE]:
        masks = masks + [m | bit for m in masks]
    masks = sorted(masks)
    n_masks = len(masks)

    n_q = min(4, local_heads)
    q_cols = q_weight.shape[1] // n_q
    n_out = max(1, min(4, out_weight.shape[1] // 128))
    out_cols = out_weight.shape[1] // n_out
    pieces = [kv_weight]
    pieces += [q_weight[:, i * q_cols : (i + 1) * q_cols] for i in range(n_q)]
    pieces += [out_weight[:, i * out_cols : (i + 1) * out_cols] for i in range(n_out)]
    high_done, y_done = [], []
    gathered = []
    firsts = []
    for i, piece in enumerate(pieces):
        blocks = {0: piece}
        for bit in high_bits:
            for m in list(blocks):
                got = swap(after(blocks[m], *high_done[-2:-1]), bit)
                high_done.append(got)
                blocks[m | bit] = got
        firsts.append(blocks)
    order = []
    for i in range(len(pieces) + 1):
        if i < len(pieces):
            order.append((i, 0))
        if i > 0:
            order += [(i - 1, m) for m in sorted(firsts[i - 1]) if m]
    for i, m in order:
        got = swap(after(firsts[i][m], *y_done[-2:-1]), Y)
        y_done.append(got)
        firsts[i][m | Y] = got
    for blocks in firsts:
        for m in list(blocks):
            blocks[m | CORE] = swap(blocks[m], CORE)
        gathered.append([blocks[m] for m in masks])

    half = width // 2
    wide = jax.ShapeDtypeStruct((rows, half), jnp.bfloat16)
    a_own, a_send = call(
        functools.partial(norm_body, masks), (wide, wide), [SM, VM, VM], 0, 3 * rows * width * 2,
        (place, tokens, norm_gain.reshape(1, width)), name="normed",
    )
    a_part = lax.dynamic_slice_in_dim(a_send, rep * (rows // n_rep), rows // n_rep, 0)
    a_recv = gather_rep(swap(a_part, SPLIT), 0)

    def project(weights, name):
        n = weights[0].shape[1]
        kept, sent = call(
            project_body,
            (jax.ShapeDtypeStruct((rows, n), jnp.float32), jax.ShapeDtypeStruct((rows, n), jnp.bfloat16)),
            [VM] * (2 + n_masks), 2 * 2 * rows * half * n, 2 * rows * half * 2 + half * n * 2,
            (a_own, a_recv, *weights), name=name,
        )
        return kept, swap(sent, SPLIT)

    middle = HEAD_SIZE // 2
    exponent = jnp.arange(middle, dtype=jnp.float32) * (2.0 / HEAD_SIZE)
    positions = (ctx * rows + jnp.arange(rows, dtype=jnp.int32)).astype(jnp.float32)
    angles = positions[:, None] * (ROPE_BASE ** (-exponent))[None, :]
    cosine, sine = jnp.cos(angles), jnp.sin(angles)
    cosine = jnp.concatenate([cosine, cosine], axis=1)
    sine = jnp.concatenate([-sine, sine], axis=1)

    kept, came = project(gathered[0], "kv_project")
    n_blocks = kv_weight.shape[1] // HEAD_SIZE
    total = kept + came.astype(jnp.float32) + kv_bias.astype(jnp.float32)
    columns = []
    for b in range(n_blocks):
        v = total[:, b * HEAD_SIZE : (b + 1) * HEAD_SIZE]
        columns.append(jnp.where(rep * n_blocks + b < KEY_VALUE_HEADS, rotate(v, cosine, sine), v))
    kv_local = jnp.concatenate(columns, axis=1).astype(jnp.bfloat16)
    key_value_cache = gather_rep(kv_local, 1)
    leading = rep * local_heads // head_group
    used = [
        lax.dynamic_slice_in_dim(key_value_cache, (first + leading) * HEAD_SIZE, kv_heads * HEAD_SIZE, 1)
        for first in (0, KEY_VALUE_HEADS)
    ]
    cache = jnp.concatenate(used, axis=1)
    for bit in [SPLIT] + high_bits + [Y, CORE]:
        cache = jnp.concatenate([cache, swap(cache, bit)], axis=0)

    heads = q_cols // HEAD_SIZE
    inner = local_heads // kv_heads
    n_tokens = rows * n_ctx
    att_own, att_recv = [], []
    for i in range(n_q):
        kept, came = project(gathered[1 + i], f"q_project{i}")
        kv_head = i * heads // inner
        keys = cache[:, kv_head * HEAD_SIZE : (kv_head + 1) * HEAD_SIZE]
        values = cache[:, (kv_heads + kv_head) * HEAD_SIZE : (kv_heads + kv_head + 1) * HEAD_SIZE]
        (attended,) = call(
            functools.partial(attend_body, n_bits),
            (jax.ShapeDtypeStruct((rows, q_cols), jnp.bfloat16),),
            [SM] + [VM] * 7, 4 * heads * rows * n_tokens * HEAD_SIZE * 2, 2 * n_tokens * HEAD_SIZE * 2,
            (place, kept, came, q_bias[i * q_cols : (i + 1) * q_cols].reshape(1, q_cols), cosine, sine, keys, values),
            scratch=[
                pltpu.VMEM((heads * rows, HEAD_SIZE), jnp.bfloat16),
                pltpu.VMEM((heads * rows, HEAD_SIZE), jnp.float32),
                pltpu.VMEM((heads * rows, 1), jnp.float32),
                pltpu.VMEM((heads * rows, 1), jnp.float32),
            ],
            name=f"attend{i}",
        )
        att_own.append(attended)
        att_recv.append(swap(attended, SPLIT))

    size = rows // n_rep
    own, recv = [], []
    for s in range(n_out):
        weights = gathered[1 + n_q + s]
        n = out_cols * n_masks
        (partial,) = call(
            functools.partial(output_body, n_q),
            (jax.ShapeDtypeStruct((n_rep, 2 * size, n), jnp.bfloat16),),
            [SM] + [VM] * (2 * n_q + n_masks), 2 * 2 * rows * out_weight.shape[0] * n,
            2 * rows * out_weight.shape[0] * 2 + out_weight.shape[0] * n * 2,
            (place, *att_own, *att_recv, *weights), name=f"out_project{s}",
        )
        total = partial[0].astype(jnp.float32)
        for far in range(1, n_rep):
            total = total + swap_rep(partial[far], far).astype(jnp.float32)
        total = total.astype(jnp.bfloat16)
        own.append(total[:size])
        recv.append(swap(total[size:], SPLIT))
    (result,) = call(
        functools.partial(place_body, masks, n_out),
        (jax.ShapeDtypeStruct((size, width), jnp.bfloat16),),
        [SM] + [VM] * (2 * n_out), 0, 2 * size * width * 2, (place, *own, *recv), name="placed",
    )
    return result, key_value_cache


def solution(mesh):
    in_specs = (
        P("ctx", None),
        P(),
        P("ctx", "rep"),
        P("rep"),
        P("ctx", "rep"),
        P("rep"),
        P("rep", "ctx"),
    )
    out_specs = (P(("ctx", "rep"), None), P("ctx", None))
    return jax.shard_map(per_device, mesh=mesh, in_specs=in_specs, out_specs=out_specs, check_vma=False)
```

time: 590 us -> 611 us (1.036); the launches traced: 587 us -> 601 us
  Pallas kernels: 0 us -> 233 us
  waiting for transfers between devices: 413 us -> 280 us
  matrix products: 104 us -> 0 us
  starting transfers between devices: 0.42 us -> 57.4 us
  other arithmetic: 39.9 us -> 11.4 us
  between operations: 15.5 us -> 1.76 us
  local copies, waits for them, and re-layouts: 4.52 us -> 17.9 us
  blocking collectives: 9.15 us -> 0 us
    all_gather x5 -> x0, waiting for transfers between devices: 356 us -> none  [the longest x1 147 us: per_device(): lax.all_gather(q_weight, 'ctx', axis=0, tiled=True)]
    ppermute x0 -> x87, waiting for transfers between devices: none -> 280 us  [the longest x81 242 us: swap(): return lax.ppermute(x, 'ctx', [(i, i ^ mask) for i in range(n)])]
    pallas_call x0 -> x15, Pallas kernels: none -> 233 us  [call(): pl.pallas_call(body, out_shape=outs, in_specs=specs, out_specs=tuple((VM...]
    dot_general x5 -> x0, matrix products: 72.2 us -> none  [the longest x2 32.2 us: attend_block(): jnp.einsum('rgjd,pgd->gjrp', query_rows, key_rows, preferred_element_type...]
    ppermute x0 -> x87, starting transfers between devices: none -> 57.4 us  [the longest x81 50.5 us: swap(): return lax.ppermute(x, 'ctx', [(i, i ^ mask) for i in range(n)])]
    reduce_scatter x1 -> x0, waiting for transfers between devices: 55.4 us -> none  [per_device(): lax.psum_scatter(terms.astype(jnp.bfloat16), 'rep', scatter_dimension=0,...]
    reduce_sum x3 -> x0, other arithmetic: 33.4 us -> none  [the longest x2 30.3 us: attend_block(): total = jnp.sum(expo, axis=-1)]
    cond x2 -> x0, matrix products: 32 us -> none  [guarded(): return lax.cond(start <= jnp.max(query_pos), active, passive, carry)]
  transfers between devices with their start and end apart: 6 -> 87, of which waited for: 6 -> 28; matrix products, arithmetic and copies ran while one was open for 22% -> 4% of each run, Pallas kernels for 0% -> 37%
where the time goes in v1:
time: 611 us; the launch traced here: 601 us
  waiting for transfers between devices  280 us (46%)
  Pallas kernels  233 us (38%)
  starting transfers between devices  57.4 us (9%)
  local copies, waits for them, and re-layouts  17.9 us (3%)
  other arithmetic  11.4 us (2%)
    ppermute x81, waiting for transfers between devices, swap(): return lax.ppermute(x, 'ctx', [(i, i ^ mask) for i in range(n)])  242 us
    pallas_call x15, Pallas kernels, call(): pl.pallas_call(body, out_shape=outs, in_specs=specs, out_specs=tuple((VM...  233 us
    ppermute x81, starting transfers between devices, swap(): return lax.ppermute(x, 'ctx', [(i, i ^ mask) for i in range(n)])  50.5 us
    ppermute x6, waiting for transfers between devices, swap_rep(): return lax.ppermute(x, 'rep', [(i, i ^ mask) for i in range(n)])  38.9 us
  transfers between devices with their start and end apart: 87, of which 28 were waited for; matrix products, arithmetic and copies ran while one was open for 4% of the time, Pallas kernels for 37%

profile of v1, /device:TPU:28, one launch (start us, length us, event | category | flops | bytes accessed | tf_op | source)
XLA Modules:
  0.0 601.4 jit_solution(1565854197798293983)
XLA Ops:
  1.5 4.7 normed.1
  8.7 35.3 %collective-permute-done = bf16[128,4096]{1,0:T(8,128)(2,1)} collective-permute-done((bf16[128,4096]{1,0:T(8,128)(2,1)S(1)}, bf16[128,4096]{1,0:T(8,128)(2,1)}, u32[]{:S(2)}, u32[]{:S(2)}) %collective-permute-start) | collective-permute-done | bytes 1048608 | tf_op jit(solution)/shard_map/ppermute | solution.py:23
  48.1 12.7 %collective-permute-done.9.refs_6_ = bf16[512,512]{1,0:T(8,128)(2,1)} collective-permute-done((bf16[512,512]{1,0:T(8,128)(2,1)}, bf16[512,512]{1,0:T(8,128)(2,1)}, u32[]{:S(2)}, u32[]{:S(2)}) %collective-permute-start.9) | collective-permute-done | bytes 524320 | tf_op jit(solution)/shard_map/ppermute | solution.py:23
  60.7 7.6 %collective-permute-done.1 = bf16[128,4096]{1,0:T(8,128)(2,1)} collective-permute-done((bf16[128,4096]{1,0:T(8,128)(2,1)}, bf16[128,4096]{1,0:T(8,128)(2,1)}, u32[]{:S(2)}, u32[]{:S(2)}) %collective-permute-start.1) | collective-permute-done | bytes 1048608 | tf_op jit(solution)/shard_map/ppermute | solution.py:28
  71.7 5.0 kv_project.1
  78.0 8.1 %collective-permute-done.17 = bf16[256,512]{1,0:T(8,128)(2,1)S(1)} collective-permute-done((bf16[256,512]{1,0:T(8,128)(2,1)S(1)}, bf16[256,512]{1,0:T(8,128)(2,1)S(1)}, u32[]{:S(2)}, u32[]{:S(2)}) %collective-permute-start.17) | collective-permute-done | bytes 262176 | tf_op jit(solution)/shard_map/ppermute | solution.py:23
  91.3 5.7 collective-permute-done.18
  99.0 27.9 %collective-permute-done.5.refs_4_ = bf16[512,512]{1,0:T(8,128)(2,1)} collective-permute-done((bf16[512,512]{1,0:T(8,128)(2,1)S(1)}, bf16[512,512]{1,0:T(8,128)(2,1)}, u32[]{:S(2)}, u32[]{:S(2)}) %collective-permute-start.5) | collective-permute-done | bytes 524320 | tf_op jit(solution)/shard_map/ppermute | solution.py:23
  127.4 16.2 %collective-permute-done.19 = bf16[256,512]{1,0:T(8,128)(2,1)S(1)} collective-permute-done((bf16[256,512]{1,0:T(8,128)(2,1)S(1)}, bf16[256,512]{1,0:T(8,128)(2,1)S(1)}, u32[]{:S(2)}, u32[]{:S(2)}) %collective-permute-start.19) | collective-permute-done | bytes 262176 | tf_op jit(solution)/shard_map/ppermute | solution.py:23
  144.7 2.9 collective-permute-start.34
  147.6 9.8 %collective-permute-done.32.refs_2_ = bf16[512,512]{1,0:T(8,128)(2,1)S(1)} collective-permute-done((bf16[512,512]{1,0:T(8,128)(2,1)S(1)}, bf16[512,512]{1,0:T(8,128)(2,1)S(1)}, u32[]{:S(2)}, u32[]{:S(2)}) %collective-permute-start.32) | collective-permute-done | bytes 524320 | tf_op jit(solution)/shard_map/ppermute | solution.py:23
  158.4 22.6 %collective-permute-done.20 = bf16[512,512]{1,0:T(8,128)(2,1)S(1)} collective-permute-done((bf16[512,512]{1,0:T(8,128)(2,1)S(1)}, bf16[512,512]{1,0:T(8,128)(2,1)S(1)}, u32[]{:S(2)}, u32[]{:S(2)}) %collective-permute-start.20) | collective-permute-done | bytes 524320 | tf_op jit(solution)/shard_map/ppermute | solution.py:23
  182.7 9.5 %collective-permute-done.34.refs_4_ = bf16[512,512]{1,0:T(8,128)(2,1)S(1)} collective-permute-done((bf16[512,512]{1,0:T(8,128)(2,1)S(1)}, bf16[512,512]{1,0:T(8,128)(2,1)S(1)}, u32[]{:S(2)}, u32[]{:S(2)}) %collective-permute-start.34) | collective-permute-done | bytes 524320 | tf_op jit(solution)/shard_map/ppermute | solution.py:23
  198.3 20.6 %collective-permute-done.42.refs_4_ = bf16[512,512]{1,0:T(8,128)(2,1)S(1)} collective-permute-done((bf16[512,512]{1,0:T(8,128)(2,1)S(1)}, bf16[512,512]{1,0:T(8,128)(2,1)S(1)}, u32[]{:S(2)}, u32[]{:S(2)}) %collective-permute-start.42) | collective-permute-done | bytes 524320 | tf_op jit(solution)/shard_map/ppermute | solution.py:23
  219.0 10.5 %collective-permute-done.36.refs_6_ = bf16[512,512]{1,0:T(8,128)(2,1)S(1)} collective-permute-done((bf16[512,512]{1,0:T(8,128)(2,1)S(1)}, bf16[512,512]{1,0:T(8,128)(2,1)S(1)}, u32[]{:S(2)}, u32[]{:S(2)}) %collective-permute-start.36) | collective-permute-done | bytes 524320 | tf_op jit(solution)/shard_map/ppermute | solution.py:23
  232.6 8.1 %collective-permute-done.52.refs_10_ = bf16[2048,128]{1,0:T(8,128)(2,1)S(1)} collective-permute-done((bf16[2048,128]{1,0:T(8,128)(2,1)S(1)}, bf16[2048,128]{1,0:T(8,128)(2,1)S(1)}, u32[]{:S(2)}, u32[]{:S(2)}) %collective-permute-start.52) | collective-permute-done | bytes 524320 | tf_op jit(solution)/shard_map/ppermute | solution.py:23
  241.5 9.4 %collective-permute-done.54.refs_12_ = bf16[2048,128]{1,0:T(8,128)(2,1)} collective-permute-done((bf16[2048,128]{1,0:T(8,128)(2,1)S(1)}, bf16[2048,128]{1,0:T(8,128)(2,1)}, u32[]{:S(2)}, u32[]{:S(2)}) %collective-permute-start.54) | collective-permute-done | bytes 524320 | tf_op jit(solution)/shard_map/ppermute | solution.py:23
  252.9 11.8 %collective-permute-done.60.refs_10_ = bf16[2048,128]{1,0:T(8,128)(2,1)S(1)} collective-permute-done((bf16[2048,128]{1,0:T(8,128)(2,1)S(1)}, bf16[2048,128]{1,0:T(8,128)(2,1)S(1)}, u32[]{:S(2)}, u32[]{:S(2)}) %collective-permute-start.60) | collective-permute-done | bytes 524320 | tf_op jit(solution)/shard_map/ppermute | solution.py:23
  266.3 12.5 %collective-permute-done.62.refs_12_ = bf16[2048,128]{1,0:T(8,128)(2,1)S(1)} collective-permute-done((bf16[2048,128]{1,0:T(8,128)(2,1)S(1)}, bf16[2048,128]{1,0:T(8,128)(2,1)S(1)}, u32[]{:S(2)}, u32[]{:S(2)}) %collective-permute-start.62) | collective-permute-done | bytes 524320 | tf_op jit(solution)/shard_map/ppermute | solution.py:23
  279.6 4.8 q_project0.1
  285.1 5.4 q_project1.1
  293.6 15.2 %q_project2.1 = (f32[256,512]{1,0:T(8,128)S(1)}, bf16[256,512]{1,0:T(8,128)(2,1)S(1)}) custom-call(bf16[256,4096]{1,0:T(8,128)(2,1)} %copy-done, bf16[256,4096]{1,0:T(8,128)(2,1)} %pad_maximum_fusion.a_recv, bf16[512,512]{1,0:T(8,128)(2,1)S(1)} %get-tuple-element.51.refs_0_, bf16[512,512]{1,0:T(8,128)(2,1)S(1)} %collective-permute-done.31.refs_1_, ...), custom_call_target="tpu_custom_call" | custom-call | flops 2147483648 | bytes 8388608 | tf_op jit(solution)/shard_map/q_project2/pallas_call | solution.py:51
  310.3 4.6 q_project3.1
  317.2 3.2 collective-permute-start.78
  320.3 3.1 constant_dynamic-update-slice_fusion
  323.5 2.6 fusion.19
  326.4 2.8 collective-permute-done.12.other
  329.2 40.5 %attend0.1.refs_0_ = bf16[256,512]{1,0:T(8,128)(2,1)S(1)} custom-call(s32[2]{0:T(128)S(1)} %pad_add_fusion.place, f32[256,512]{1,0:T(8,128)S(1)} %copy-done.17, bf16[256,512]{1,0:T(8,128)(2,1)S(1)} %collective-permute-done.12.other, bf16[1,512]{1,0:T(2,128)(2,1)S(1)} %reshape.40.bias, f32[256,128]{1,0:T(8,128)S(1)} %get-tuple-element.113.cosine, ...), custom_call_target="tpu_custom_call" | custom-call | flops 4294967296 | bytes 2097152 | tf_op jit(solution)/shard_map/attend0/pallas_call | solution.py:51
  369.8 3.3 collective-permute-start.61
  373.3 40.6 %attend1.1.refs_1_ = bf16[256,512]{1,0:T(8,128)(2,1)S(1)} custom-call(s32[2]{0:T(128)S(1)} %pad_add_fusion.place, f32[256,512]{1,0:T(8,128)S(1)} %get-tuple-element.48.mine, bf16[256,512]{1,0:T(8,128)(2,1)S(1)} %collective-permute-done.30.other, bf16[1,512]{1,0:T(2,128)(2,1)S(1)} %reshape.41.bias, f32[256,128]{1,0:T(8,128)S(1)} %get-tuple-element.113.cosine, ...), custom_call_target="tpu_custom_call" | custom-call | flops 4294967296 | bytes 2097152 | tf_op jit(solution)/shard_map/attend1/pallas_call | solution.py:51
  414.0 3.2 collective-permute-start.65
  417.2 40.5 %attend2.1.refs_2_ = bf16[256,512]{1,0:T(8,128)(2,1)S(1)} custom-call(s32[2]{0:T(128)S(1)} %pad_add_fusion.place, f32[256,512]{1,0:T(8,128)S(1)} %get-tuple-element.53.mine, bf16[256,512]{1,0:T(8,128)(2,1)S(1)} %collective-permute-done.38.other, bf16[1,512]{1,0:T(2,128)(2,1)S(1)} %reshape.42.bias, f32[256,128]{1,0:T(8,128)S(1)} %get-tuple-element.113.cosine, ...), custom_call_target="tpu_custom_call" | custom-call | flops 4294967296 | bytes 2097152 | tf_op jit(solution)/shard_map/attend2/pallas_call | solution.py:51
  460.1 40.9 %attend3.1.refs_3_ = bf16[256,512]{1,0:T(8,128)(2,1)S(1)} custom-call(s32[2]{0:T(128)S(1)} %pad_add_fusion.place, f32[256,512]{1,0:T(8,128)S(1)} %get-tuple-element.58.mine, bf16[256,512]{1,0:T(8,128)(2,1)S(1)} %collective-permute-done.46.other, bf16[1,512]{1,0:T(2,128)(2,1)S(1)} %reshape.43.bias, f32[256,128]{1,0:T(8,128)S(1)} %get-tuple-element.113.cosine, ...), custom_call_target="tpu_custom_call" | custom-call | flops 4294967296 | bytes 2097152 | tf_op jit(solution)/shard_map/attend3/pallas_call | solution.py:51
  501.1 5.0 collective-permute-start.67
  507.5 4.1 collective-permute-start.73
  511.6 7.0 %out_project0.1 = bf16[2,256,1024]{2,1,0:T(8,128)(2,1)} custom-call(s32[2]{0:T(128)S(1)} %pad_add_fusion.place, bf16[256,512]{1,0:T(8,128)(2,1)S(1)} %attend0.1.refs_0_, bf16[256,512]{1,0:T(8,128)(2,1)S(1)} %attend1.1.refs_1_, bf16[256,512]{1,0:T(8,128)(2,1)S(1)} %attend2.1.refs_2_, bf16[256,512]{1,0:T(8,128)(2,1)S(1)} %attend3.1.refs_3_, ...), custom_call_target="tpu_custom_call" | custom-call | flops 2147483648 | bytes 6291456 | tf_op jit(solution)/shard_map/out_project0/pallas_call | solution.py:51
  518.6 6.9 %out_project1.1 = bf16[2,256,1024]{2,1,0:T(8,128)(2,1)} custom-call(s32[2]{0:T(128)S(1)} %pad_add_fusion.place, bf16[256,512]{1,0:T(8,128)(2,1)S(1)} %attend0.1.refs_0_, bf16[256,512]{1,0:T(8,128)(2,1)S(1)} %attend1.1.refs_1_, bf16[256,512]{1,0:T(8,128)(2,1)S(1)} %attend2.1.refs_2_, bf16[256,512]{1,0:T(8,128)(2,1)S(1)} %attend3.1.refs_3_, ...), custom_call_target="tpu_custom_call" | custom-call | flops 2147483648 | bytes 6291456 | tf_op jit(solution)/shard_map/out_project1/pallas_call | solution.py:51
  527.4 7.2 %out_project2.1 = bf16[2,256,1024]{2,1,0:T(8,128)(2,1)} custom-call(s32[2]{0:T(128)S(1)} %pad_add_fusion.place, bf16[256,512]{1,0:T(8,128)(2,1)S(1)} %attend0.1.refs_0_, bf16[256,512]{1,0:T(8,128)(2,1)S(1)} %attend1.1.refs_1_, bf16[256,512]{1,0:T(8,128)(2,1)S(1)} %attend2.1.refs_2_, bf16[256,512]{1,0:T(8,128)(2,1)S(1)} %attend3.1.refs_3_, ...), custom_call_target="tpu_custom_call" | custom-call | flops 2147483648 | bytes 6291456 | tf_op jit(solution)/shard_map/out_project2/pallas_call | solution.py:51
  538.6 6.8 %out_project3.1 = bf16[2,256,1024]{2,1,0:T(8,128)(2,1)} custom-call(s32[2]{0:T(128)S(1)} %pad_add_fusion.place, bf16[256,512]{1,0:T(8,128)(2,1)S(1)} %attend0.1.refs_0_, bf16[256,512]{1,0:T(8,128)(2,1)S(1)} %attend1.1.refs_1_, bf16[256,512]{1,0:T(8,128)(2,1)S(1)} %attend2.1.refs_2_, bf16[256,512]{1,0:T(8,128)(2,1)S(1)} %attend3.1.refs_3_, ...), custom_call_target="tpu_custom_call" | custom-call | flops 2147483648 | bytes 6291456 | tf_op jit(solution)/shard_map/out_project3/pallas_call | solution.py:51
  548.1 4.5 collective-permute-done.66
  552.9 11.0 %collective-permute-done.74 = bf16[256,1024]{1,0:T(8,128)(2,1)S(1)} collective-permute-done((bf16[256,1024]{1,0:T(8,128)(2,1)S(1)}, bf16[256,1024]{1,0:T(8,128)(2,1)S(1)}, u32[]{:S(2)}, u32[]{:S(2)}) %collective-permute-start.74) | collective-permute-done | bytes 524320 | tf_op jit(solution)/shard_map/ppermute | solution.py:28
  564.1 10.1 %collective-permute-done.82 = bf16[256,1024]{1,0:T(8,128)(2,1)S(1)} collective-permute-done((bf16[256,1024]{1,0:T(8,128)(2,1)S(1)}, bf16[256,1024]{1,0:T(8,128)(2,1)S(1)}, u32[]{:S(2)}, u32[]{:S(2)}) %collective-permute-start.82) | collective-permute-done | bytes 524320 | tf_op jit(solution)/shard_map/ppermute | solution.py:28
  574.5 2.0 collective-permute-start.84
  579.5 4.3 collective-permute-done.83.refs_4_
  583.8 5.6 collective-permute-done.84.refs_5_
  589.4 5.6 collective-permute-done.85.refs_6_
  595.0 3.8 collective-permute-done.86.refs_7_
  598.8 2.4 placed.1
  (270 shorter events, 61.6 us)
Async XLA Ops:
  7.7 36.3 %collective-permute-start = (bf16[128,4096]{1,0:T(8,128)(2,1)S(1)}, bf16[128,4096]{1,0:T(8,128)(2,1)}, u32[]{:S(2)}, u32[]{:S(2)}) collective-permute-start(bf16[128,4096]{1,0:T(8,128)(2,1)S(1)} %constant_dynamic-slice_fusion), channel_id=1, source_target_pairs={{0,8},{2,10},{4,12},{6,14},{8,0},{10,2},{12,4},{14,6},{16,24},{18,... | collective-permute-start | bytes 3145736 | tf_op jit(solution)/shard_map/ppermute | solution.py:23
  8.2 37.3 %collective-permute-start.7 = (bf16[512,512]{1,0:T(8,128)(2,1)S(1)}, bf16[512,512]{1,0:T(8,128)(2,1)}, u32[]{:S(2)}, u32[]{:S(2)}) collective-permute-start(bf16[512,512]{1,0:T(8,128)(2,1)S(1)} %copy-done.1), channel_id=1, source_target_pairs={{0,16},{2,18},{4,20},{6,22},{8,24},{10,26},{12,28},{14,30},{16,0},... | collective-permute-start | bytes 1572872 | tf_op jit(solution)/shard_map/ppermute | solution.py:23
  8.5 36.9 %collective-permute-start.8 = (bf16[512,512]{1,0:T(8,128)(2,1)S(1)}, bf16[512,512]{1,0:T(8,128)(2,1)S(1)}, u32[]{:S(2)}, u32[]{:S(2)}) collective-permute-start(bf16[512,512]{1,0:T(8,128)(2,1)S(1)} %copy-done.1), channel_id=1, source_target_pairs={{0,4},{2,6},{4,0},{6,2},{8,12},{10,14},{12,8},{14,10},{16,20},{18,... | collective-permute-start | bytes 1572872 | tf_op jit(solution)/shard_map/ppermute | solution.py:23
  44.0 24.4 %collective-permute-start.1 = (bf16[128,4096]{1,0:T(8,128)(2,1)}, bf16[128,4096]{1,0:T(8,128)(2,1)}, u32[]{:S(2)}, u32[]{:S(2)}) collective-permute-start(bf16[128,4096]{1,0:T(8,128)(2,1)} %collective-permute-done), channel_id=1, source_target_pairs={{0,1},{1,0},{2,3},{3,2},{4,5},{5,4},{6,7},{7,6},{8,9},{9,8},{10,11... | collective-permute-start | bytes 3145736 | tf_op jit(solution)/shard_map/ppermute | solution.py:28
  46.3 25.3 %collective-permute-start.13 = (bf16[512,512]{1,0:T(8,128)(2,1)S(1)}, bf16[512,512]{1,0:T(8,128)(2,1)}, u32[]{:S(2)}, u32[]{:S(2)}) collective-permute-start(bf16[512,512]{1,0:T(8,128)(2,1)S(1)} %copy-done.1), channel_id=1, source_target_pairs={{0,2},{2,0},{4,6},{6,4},{8,10},{10,8},{12,14},{14,12},{16,18},{18,... | collective-permute-start | bytes 1572872 | tf_op jit(solution)/shard_map/ppermute | solution.py:23
  46.5 43.7 %collective-permute-start.3 = (bf16[512,512]{1,0:T(8,128)(2,1)S(1)}, bf16[512,512]{1,0:T(8,128)(2,1)S(1)}, u32[]{:S(2)}, u32[]{:S(2)}) collective-permute-start(bf16[512,512]{1,0:T(8,128)(2,1)S(1)} %get-tuple-element.84.refs_0_), channel_id=1, source_target_pairs={{0,4},{2,6},{4,0},{6,2},{8,12},{10,14},{12,8},{14,10},{16,20},{18,... | collective-permute-start | bytes 1572872 | tf_op jit(solution)/shard_map/ppermute | solution.py:23
  47.9 23.8 %collective-permute-start.14 = (bf16[512,512]{1,0:T(8,128)(2,1)}, bf16[512,512]{1,0:T(8,128)(2,1)S(1)}, u32[]{:S(2)}, u32[]{:S(2)}) collective-permute-start(bf16[512,512]{1,0:T(8,128)(2,1)} %copy-done.2), channel_id=1, source_target_pairs={{0,2},{2,0},{4,6},{6,4},{8,10},{10,8},{12,14},{14,12},{16,18},{18,... | collective-permute-start | bytes 1572872 | tf_op jit(solution)/shard_map/ppermute | solution.py:23
  90.2 36.8 %collective-permute-start.5 = (bf16[512,512]{1,0:T(8,128)(2,1)S(1)}, bf16[512,512]{1,0:T(8,128)(2,1)}, u32[]{:S(2)}, u32[]{:S(2)}) collective-permute-start(bf16[512,512]{1,0:T(8,128)(2,1)S(1)} %get-tuple-element.84.refs_0_), channel_id=1, source_target_pairs={{0,16},{2,18},{4,20},{6,22},{8,24},{10,26},{12,28},{14,30},{16,0},... | collective-permute-start | bytes 1572872 | tf_op jit(solution)/shard_map/ppermute | solution.py:23
  90.2 36.8 %collective-permute-start.24 = (bf16[512,512]{1,0:T(8,128)(2,1)S(1)}, bf16[512,512]{1,0:T(8,128)(2,1)S(1)}, u32[]{:S(2)}, u32[]{:S(2)}) collective-permute-start(bf16[512,512]{1,0:T(8,128)(2,1)S(1)} %get-tuple-element.46.refs_0_), channel_id=1, source_target_pairs={{0,4},{2,6},{4,0},{6,2},{8,12},{10,14},{12,8},{14,10},{16,20},{18,... | collective-permute-start | bytes 1572872 | tf_op jit(solution)/shard_map/ppermute | solution.py:23
  90.7 53.4 %collective-permute-start.2 = (bf16[512,512]{1,0:T(8,128)(2,1)S(1)}, bf16[512,512]{1,0:T(8,128)(2,1)}, u32[]{:S(2)}, u32[]{:S(2)}) collective-permute-start(bf16[512,512]{1,0:T(8,128)(2,1)S(1)} %get-tuple-element.84.refs_0_), channel_id=1, source_target_pairs={{0,2},{2,0},{4,6},{6,4},{8,10},{10,8},{12,14},{14,12},{16,18},{18,... | collective-permute-start | bytes 1572872 | tf_op jit(solution)/shard_map/ppermute | solution.py:23
  90.7 53.5 %collective-permute-start.23 = (bf16[512,512]{1,0:T(8,128)(2,1)S(1)}, bf16[512,512]{1,0:T(8,128)(2,1)}, u32[]{:S(2)}, u32[]{:S(2)}) collective-permute-start(bf16[512,512]{1,0:T(8,128)(2,1)S(1)} %get-tuple-element.46.refs_0_), channel_id=1, source_target_pairs={{0,2},{2,0},{4,6},{6,4},{8,10},{10,8},{12,14},{14,12},{16,18},{18,... | collective-permute-start | bytes 1572872 | tf_op jit(solution)/shard_map/ppermute | solution.py:23
  96.9 47.8 %collective-permute-start.26 = (bf16[512,512]{1,0:T(8,128)(2,1)S(1)}, bf16[512,512]{1,0:T(8,128)(2,1)S(1)}, u32[]{:S(2)}, u32[]{:S(2)}) collective-permute-start(bf16[512,512]{1,0:T(8,128)(2,1)S(1)} %get-tuple-element.46.refs_0_), channel_id=1, source_target_pairs={{0,16},{2,18},{4,20},{6,22},{8,24},{10,26},{12,28},{14,30},{16,0},... | collective-permute-start | bytes 1572872 | tf_op jit(solution)/shard_map/ppermute | solution.py:23
  144.7 36.3 %collective-permute-start.20 = (bf16[512,512]{1,0:T(8,128)(2,1)S(1)}, bf16[512,512]{1,0:T(8,128)(2,1)S(1)}, u32[]{:S(2)}, u32[]{:S(2)}) collective-permute-start(bf16[512,512]{1,0:T(8,128)(2,1)S(1)} %pad_maximum_fusion.4), channel_id=1, source_target_pairs={{0,16},{2,18},{4,20},{6,22},{8,24},{10,26},{12,28},{14,30},{16,0},... | collective-permute-start | bytes 1572872 | tf_op jit(solution)/shard_map/ppermute | solution.py:23
  144.7 47.5 %collective-permute-start.34 = (bf16[512,512]{1,0:T(8,128)(2,1)S(1)}, bf16[512,512]{1,0:T(8,128)(2,1)S(1)}, u32[]{:S(2)}, u32[]{:S(2)}) collective-permute-start(bf16[512,512]{1,0:T(8,128)(2,1)S(1)} %get-tuple-element.51.refs_0_), channel_id=1, source_target_pairs={{0,16},{2,18},{4,20},{6,22},{8,24},{10,26},{12,28},{14,30},{16,0},... | collective-permute-start | bytes 1572872 | tf_op jit(solution)/shard_map/ppermute | solution.py:23
  157.4 36.3 %collective-permute-start.28 = (bf16[512,512]{1,0:T(8,128)(2,1)S(1)}, bf16[512,512]{1,0:T(8,128)(2,1)S(1)}, u32[]{:S(2)}, u32[]{:S(2)}) collective-permute-start(bf16[512,512]{1,0:T(8,128)(2,1)S(1)} %collective-permute-done.26.refs_4_), channel_id=1, source_target_pairs={{0,4},{2,6},{4,0},{6,2},{8,12},{10,14},{12,8},{14,10},{16,20},{18,... | collective-permute-start | bytes 1572872 | tf_op jit(solution)/shard_map/ppermute | solution.py:23
  157.9 35.8 %collective-permute-start.4 = (bf16[512,512]{1,0:T(8,128)(2,1)S(1)}, bf16[512,512]{1,0:T(8,128)(2,1)S(1)}, u32[]{:S(2)}, u32[]{:S(2)}) collective-permute-start(bf16[512,512]{1,0:T(8,128)(2,1)S(1)} %collective-permute-done.3.refs_2_), channel_id=1, source_target_pairs={{0,2},{2,0},{4,6},{6,4},{8,10},{10,8},{12,14},{14,12},{16,18},{18,... | collective-permute-start | bytes 1572872 | tf_op jit(solution)/shard_map/ppermute | solution.py:23
  157.9 35.9 %collective-permute-start.6 = (bf16[512,512]{1,0:T(8,128)(2,1)}, bf16[512,512]{1,0:T(8,128)(2,1)S(1)}, u32[]{:S(2)}, u32[]{:S(2)}) collective-permute-start(bf16[512,512]{1,0:T(8,128)(2,1)} %collective-permute-done.5.refs_4_), channel_id=1, source_target_pairs={{0,2},{2,0},{4,6},{6,4},{8,10},{10,8},{12,14},{14,12},{16,18},{18,... | collective-permute-start | bytes 1572872 | tf_op jit(solution)/shard_map/ppermute | solution.py:23
  192.2 37.3 %collective-permute-start.21 = (bf16[1024,512]{1,0:T(8,128)(2,1)S(1)}, bf16[1024,512]{1,0:T(8,128)(2,1)S(1)}, u32[]{:S(2)}, u32[]{:S(2)}) collective-permute-start(bf16[1024,512]{1,0:T(8,128)(2,1)S(1)} %pad_maximum_fusion.2), channel_id=1, source_target_pairs={{0,4},{2,6},{4,0},{6,2},{8,12},{10,14},{12,8},{14,10},{16,20},{18,... | collective-permute-start | bytes 3145736 | tf_op jit(solution)/shard_map/ppermute | solution.py:23
  193.8 25.1 %collective-permute-start.42 = (bf16[512,512]{1,0:T(8,128)(2,1)S(1)}, bf16[512,512]{1,0:T(8,128)(2,1)S(1)}, u32[]{:S(2)}, u32[]{:S(2)}) collective-permute-start(bf16[512,512]{1,0:T(8,128)(2,1)S(1)} %get-tuple-element.56.refs_0_), channel_id=1, source_target_pairs={{0,16},{2,18},{4,20},{6,22},{8,24},{10,26},{12,28},{14,30},{16,0},... | collective-permute-start | bytes 1572872 | tf_op jit(solution)/shard_map/ppermute | solution.py:23
  193.8 35.6 %collective-permute-start.27 = (bf16[512,512]{1,0:T(8,128)(2,1)S(1)}, bf16[512,512]{1,0:T(8,128)(2,1)S(1)}, u32[]{:S(2)}, u32[]{:S(2)}) collective-permute-start(bf16[512,512]{1,0:T(8,128)(2,1)S(1)} %collective-permute-done.26.refs_4_), channel_id=1, source_target_pairs={{0,2},{2,0},{4,6},{6,4},{8,10},{10,8},{12,14},{14,12},{16,18},{18,... | collective-permute-start | bytes 1572872 | tf_op jit(solution)/shard_map/ppermute | solution.py:23
  194.8 34.6 %collective-permute-start.36 = (bf16[512,512]{1,0:T(8,128)(2,1)S(1)}, bf16[512,512]{1,0:T(8,128)(2,1)S(1)}, u32[]{:S(2)}, u32[]{:S(2)}) collective-permute-start(bf16[512,512]{1,0:T(8,128)(2,1)S(1)} %collective-permute-done.34.refs_4_), channel_id=1, source_target_pairs={{0,4},{2,6},{4,0},{6,2},{8,12},{10,14},{12,8},{14,10},{16,20},{18,... | collective-permute-start | bytes 1572872 | tf_op jit(solution)/shard_map/ppermute | solution.py:23
  197.7 43.0 %collective-permute-start.52 = (bf16[2048,128]{1,0:T(8,128)(2,1)S(1)}, bf16[2048,128]{1,0:T(8,128)(2,1)S(1)}, u32[]{:S(2)}, u32[]{:S(2)}) collective-permute-start(bf16[2048,128]{1,0:T(8,128)(2,1)S(1)} %get-tuple-element.61.refs_8_), channel_id=1, source_target_pairs={{0,4},{2,6},{4,0},{6,2},{8,12},{10,14},{12,8},{14,10},{16,20},{18,... | collective-permute-start | bytes 1572872 | tf_op jit(solution)/shard_map/ppermute | solution.py:23
  240.7 76.5 %collective-permute-start.22 = (bf16[2048,512]{1,0:T(8,128)(2,1)}, bf16[2048,512]{1,0:T(8,128)(2,1)}, u32[]{:S(2)}, u32[]{:S(2)}) collective-permute-start(bf16[2048,512]{1,0:T(8,128)(2,1)} %pad_maximum_fusion.1), channel_id=1, source_target_pairs={{0,2},{2,0},{4,6},{6,4},{8,10},{10,8},{12,14},{14,12},{16,18},{18,... | collective-permute-start | bytes 6291464 | tf_op jit(solution)/shard_map/ppermute | solution.py:23
  252.4 26.5 %collective-permute-start.62 = (bf16[2048,128]{1,0:T(8,128)(2,1)S(1)}, bf16[2048,128]{1,0:T(8,128)(2,1)S(1)}, u32[]{:S(2)}, u32[]{:S(2)}) collective-permute-start(bf16[2048,128]{1,0:T(8,128)(2,1)S(1)} %get-tuple-element.64.refs_8_), channel_id=1, source_target_pairs={{0,16},{2,18},{4,20},{6,22},{8,24},{10,26},{12,28},{14,30},{16,0},... | collective-permute-start | bytes 1572872 | tf_op jit(solution)/shard_map/ppermute | solution.py:23
  252.5 32.0 %collective-permute-start.29 = (bf16[512,512]{1,0:T(8,128)(2,1)S(1)}, bf16[512,512]{1,0:T(8,128)(2,1)S(1)}, u32[]{:S(2)}, u32[]{:S(2)}) collective-permute-start(bf16[512,512]{1,0:T(8,128)(2,1)S(1)} %collective-permute-done.28.refs_6_), channel_id=1, source_target_pairs={{0,2},{2,0},{4,6},{6,4},{8,10},{10,8},{12,14},{14,12},{16,18},{18,... | collective-permute-start | bytes 1572872 | tf_op jit(solution)/shard_map/ppermute | solution.py:23
  266.2 25.0 %collective-permute-start.37 = (bf16[512,512]{1,0:T(8,128)(2,1)S(1)}, bf16[512,512]{1,0:T(8,128)(2,1)S(1)}, u32[]{:S(2)}, u32[]{:S(2)}) collective-permute-start(bf16[512,512]{1,0:T(8,128)(2,1)S(1)} %collective-permute-done.36.refs_6_), channel_id=1, source_target_pairs={{0,2},{2,0},{4,6},{6,4},{8,10},{10,8},{12,14},{14,12},{16,18},{18,... | collective-permute-start | bytes 1572872 | tf_op jit(solution)/shard_map/ppermute | solution.py:23
  284.5 25.2 %collective-permute-start.41 = (bf16[512,512]{1,0:T(8,128)(2,1)S(1)}, bf16[512,512]{1,0:T(8,128)(2,1)S(1)}, u32[]{:S(2)}, u32[]{:S(2)}) collective-permute-start(bf16[512,512]{1,0:T(8,128)(2,1)S(1)} %collective-permute-done.40.refs_2_), channel_id=1, source_target_pairs={{0,2},{2,0},{4,6},{6,4},{8,10},{10,8},{12,14},{14,12},{16,18},{18,... | collective-permute-start | bytes 1572872 | tf_op jit(solution)/shard_map/ppermute | solution.py:23
  284.7 25.1 %collective-permute-start.45 = (bf16[512,512]{1,0:T(8,128)(2,1)S(1)}, bf16[512,512]{1,0:T(8,128)(2,1)S(1)}, u32[]{:S(2)}, u32[]{:S(2)}) collective-permute-start(bf16[512,512]{1,0:T(8,128)(2,1)S(1)} %collective-permute-done.44.refs_6_), channel_id=1, source_target_pairs={{0,2},{2,0},{4,6},{6,4},{8,10},{10,8},{12,14},{14,12},{16,18},{18,... | collective-permute-start | bytes 1572872 | tf_op jit(solution)/shard_map/ppermute | solution.py:23
  291.2 24.9 %collective-permute-start.70 = (bf16[2048,128]{1,0:T(8,128)(2,1)}, bf16[2048,128]{1,0:T(8,128)(2,1)S(1)}, u32[]{:S(2)}, u32[]{:S(2)}) collective-permute-start(bf16[2048,128]{1,0:T(8,128)(2,1)} %get-tuple-element.67.refs_8_), channel_id=1, source_target_pairs={{0,16},{2,18},{4,20},{6,22},{8,24},{10,26},{12,28},{14,30},{16,0},... | collective-permute-start | bytes 1572872 | tf_op jit(solution)/shard_map/ppermute | solution.py:23
  293.0 23.1 %collective-permute-start.64 = (bf16[2048,128]{1,0:T(8,128)(2,1)S(1)}, bf16[2048,128]{1,0:T(8,128)(2,1)S(1)}, u32[]{:S(2)}, u32[]{:S(2)}) collective-permute-start(bf16[2048,128]{1,0:T(8,128)(2,1)S(1)} %copy-done.15), channel_id=1, source_target_pairs={{0,4},{2,6},{4,0},{6,2},{8,12},{10,14},{12,8},{14,10},{16,20},{18,... | collective-permute-start | bytes 1572872 | tf_op jit(solution)/shard_map/ppermute | solution.py:23
  316.1 53.6 %collective-permute-start.55 = (bf16[2048,128]{1,0:T(8,128)(2,1)}, bf16[2048,128]{1,0:T(8,128)(2,1)S(1)}, u32[]{:S(2)}, u32[]{:S(2)}) collective-permute-start(bf16[2048,128]{1,0:T(8,128)(2,1)} %collective-permute-done.54.refs_12_), channel_id=1, source_target_pairs={{0,2},{2,0},{4,6},{6,4},{8,10},{10,8},{12,14},{14,12},{16,18},{18,... | collective-permute-start | bytes 1572872 | tf_op jit(solution)/shard_map/ppermute | solution.py:23
  317.2 56.0 %collective-permute-start.78 = (bf16[2048,128]{1,0:T(8,128)(2,1)S(1)}, bf16[2048,128]{1,0:T(8,128)(2,1)S(1)}, u32[]{:S(2)}, u32[]{:S(2)}) collective-permute-start(bf16[2048,128]{1,0:T(8,128)(2,1)S(1)} %copy-done.5), channel_id=1, source_target_pairs={{0,16},{2,18},{4,20},{6,22},{8,24},{10,26},{12,28},{14,30},{16,0},... | collective-permute-start | bytes 1572872 | tf_op jit(solution)/shard_map/ppermute | solution.py:23
  323.4 46.4 %collective-permute-start.63 = (bf16[2048,128]{1,0:T(8,128)(2,1)S(1)}, bf16[2048,128]{1,0:T(8,128)(2,1)S(1)}, u32[]{:S(2)}, u32[]{:S(2)}) collective-permute-start(bf16[2048,128]{1,0:T(8,128)(2,1)S(1)} %copy-done.15), channel_id=1, source_target_pairs={{0,2},{2,0},{4,6},{6,4},{8,10},{10,8},{12,14},{14,12},{16,18},{18,... | collective-permute-start | bytes 1572872 | tf_op jit(solution)/shard_map/ppermute | solution.py:23
  326.1 47.0 %collective-permute-start.30 = (bf16[256,512]{1,0:T(8,128)(2,1)}, bf16[256,512]{1,0:T(8,128)(2,1)S(1)}, u32[]{:S(2)}, u32[]{:S(2)}) collective-permute-start(bf16[256,512]{1,0:T(8,128)(2,1)} %get-tuple-element.49), channel_id=1, source_target_pairs={{0,8},{2,10},{4,12},{6,14},{8,0},{10,2},{12,4},{14,6},{16,24},{18,... | collective-permute-start | bytes 786440 | tf_op jit(solution)/shard_map/ppermute | solution.py:23
  329.1 84.7 %collective-permute-start.53 = (bf16[2048,128]{1,0:T(8,128)(2,1)S(1)}, bf16[2048,128]{1,0:T(8,128)(2,1)S(1)}, u32[]{:S(2)}, u32[]{:S(2)}) collective-permute-start(bf16[2048,128]{1,0:T(8,128)(2,1)S(1)} %copy-done.11), channel_id=1, source_target_pairs={{0,2},{2,0},{4,6},{6,4},{8,10},{10,8},{12,14},{14,12},{16,18},{18,... | collective-permute-start | bytes 1572872 | tf_op jit(solution)/shard_map/ppermute | solution.py:23
  369.7 44.2 %collective-permute-start.38 = (bf16[256,512]{1,0:T(8,128)(2,1)S(1)}, bf16[256,512]{1,0:T(8,128)(2,1)S(1)}, u32[]{:S(2)}, u32[]{:S(2)}) collective-permute-start(bf16[256,512]{1,0:T(8,128)(2,1)S(1)} %get-tuple-element.54), channel_id=1, source_target_pairs={{0,8},{2,10},{4,12},{6,14},{8,0},{10,2},{12,4},{14,6},{16,24},{18,... | collective-permute-start | bytes 786440 | tf_op jit(solution)/shard_map/ppermute | solution.py:23
  369.8 87.9 %collective-permute-start.61 = (bf16[2048,128]{1,0:T(8,128)(2,1)S(1)}, bf16[2048,128]{1,0:T(8,128)(2,1)S(1)}, u32[]{:S(2)}, u32[]{:S(2)}) collective-permute-start(bf16[2048,128]{1,0:T(8,128)(2,1)S(1)} %copy-done.13), channel_id=1, source_target_pairs={{0,2},{2,0},{4,6},{6,4},{8,10},{10,8},{12,14},{14,12},{16,18},{18,... | collective-permute-start | bytes 1572872 | tf_op jit(solution)/shard_map/ppermute | solution.py:23
  373.1 86.8 %collective-permute-start.76 = (bf16[2048,128]{1,0:T(8,128)(2,1)S(1)}, bf16[2048,128]{1,0:T(8,128)(2,1)S(1)}, u32[]{:S(2)}, u32[]{:S(2)}) collective-permute-start(bf16[2048,128]{1,0:T(8,128)(2,1)S(1)} %copy-done.5), channel_id=1, source_target_pairs={{0,4},{2,6},{4,0},{6,2},{8,12},{10,14},{12,8},{14,10},{16,20},{18,... | collective-permute-start | bytes 1572872 | tf_op jit(solution)/shard_map/ppermute | solution.py:23
  373.2 84.8 %collective-permute-start.57 = (bf16[2048,128]{1,0:T(8,128)(2,1)}, bf16[2048,128]{1,0:T(8,128)(2,1)S(1)}, u32[]{:S(2)}, u32[]{:S(2)}) collective-permute-start(bf16[2048,128]{1,0:T(8,128)(2,1)} %collective-permute-done.56.refs_14_), channel_id=1, source_target_pairs={{0,2},{2,0},{4,6},{6,4},{8,10},{10,8},{12,14},{14,12},{16,18},{18,... | collective-permute-start | bytes 1572872 | tf_op jit(solution)/shard_map/ppermute | solution.py:23
  413.9 44.0 %collective-permute-start.46 = (bf16[256,512]{1,0:T(8,128)(2,1)S(1)}, bf16[256,512]{1,0:T(8,128)(2,1)S(1)}, u32[]{:S(2)}, u32[]{:S(2)}) collective-permute-start(bf16[256,512]{1,0:T(8,128)(2,1)S(1)} %get-tuple-element.59), channel_id=1, source_target_pairs={{0,8},{2,10},{4,12},{6,14},{8,0},{10,2},{12,4},{14,6},{16,24},{18,... | collective-permute-start | bytes 786440 | tf_op jit(solution)/shard_map/ppermute | solution.py:23
  414.0 87.0 %collective-permute-start.65 = (bf16[2048,128]{1,0:T(8,128)(2,1)S(1)}, bf16[2048,128]{1,0:T(8,128)(2,1)S(1)}, u32[]{:S(2)}, u32[]{:S(2)}) collective-permute-start(bf16[2048,128]{1,0:T(8,128)(2,1)S(1)} %collective-permute-done.64.refs_14_), channel_id=1, source_target_pairs={{0,2},{2,0},{4,6},{6,4},{8,10},{10,8},{12,14},{14,12},{16,18},{18,... | collective-permute-start | bytes 1572872 | tf_op jit(solution)/shard_map/ppermute | solution.py:23
  457.8 43.3 %collective-permute-start.72 = (bf16[2048,128]{1,0:T(8,128)(2,1)S(1)}, bf16[2048,128]{1,0:T(8,128)(2,1)S(1)}, u32[]{:S(2)}, u32[]{:S(2)}) collective-permute-start(bf16[2048,128]{1,0:T(8,128)(2,1)S(1)} %collective-permute-done.70.refs_12_), channel_id=1, source_target_pairs={{0,4},{2,6},{4,0},{6,2},{8,12},{10,14},{12,8},{14,10},{16,20},{18,... | collective-permute-start | bytes 1572872 | tf_op jit(solution)/shard_map/ppermute | solution.py:23
  457.9 48.3 %collective-permute-start.47 = (bf16[256,512]{1,0:T(8,128)(2,1)S(1)}, bf16[256,512]{1,0:T(8,128)(2,1)S(1)}, u32[]{:S(2)}, u32[]{:S(2)}) collective-permute-start(bf16[256,512]{1,0:T(8,128)(2,1)S(1)} %attend0.1.refs_0_), channel_id=1, source_target_pairs={{0,8},{2,10},{4,12},{6,14},{8,0},{10,2},{12,4},{14,6},{16,24},{18,... | collective-permute-start | bytes 786440 | tf_op jit(solution)/shard_map/ppermute | solution.py:23
  458.0 48.3 %collective-permute-start.48 = (bf16[256,512]{1,0:T(8,128)(2,1)S(1)}, bf16[256,512]{1,0:T(8,128)(2,1)S(1)}, u32[]{:S(2)}, u32[]{:S(2)}) collective-permute-start(bf16[256,512]{1,0:T(8,128)(2,1)S(1)} %attend1.1.refs_1_), channel_id=1, source_target_pairs={{0,8},{2,10},{4,12},{6,14},{8,0},{10,2},{12,4},{14,6},{16,24},{18,... | collective-permute-start | bytes 786440 | tf_op jit(solution)/shard_map/ppermute | solution.py:23
  460.0 46.7 %collective-permute-start.49 = (bf16[256,512]{1,0:T(8,128)(2,1)S(1)}, bf16[256,512]{1,0:T(8,128)(2,1)S(1)}, u32[]{:S(2)}, u32[]{:S(2)}) collective-permute-start(bf16[256,512]{1,0:T(8,128)(2,1)S(1)} %attend2.1.refs_2_), channel_id=1, source_target_pairs={{0,8},{2,10},{4,12},{6,14},{8,0},{10,2},{12,4},{14,6},{16,24},{18,... | collective-permute-start | bytes 786440 | tf_op jit(solution)/shard_map/ppermute | solution.py:23
  501.1 24.4 %collective-permute-start.67 = (bf16[2048,128]{1,0:T(8,128)(2,1)}, bf16[2048,128]{1,0:T(8,128)(2,1)S(1)}, u32[]{:S(2)}, u32[]{:S(2)}) collective-permute-start(bf16[2048,128]{1,0:T(8,128)(2,1)} %get-tuple-element.67.refs_8_), channel_id=1, source_target_pairs={{0,2},{2,0},{4,6},{6,4},{8,10},{10,8},{12,14},{14,12},{16,18},{18,... | collective-permute-start | bytes 1572872 | tf_op jit(solution)/shard_map/ppermute | solution.py:23
  537.0 26.8 %collective-permute-start.74 = (bf16[256,1024]{1,0:T(8,128)(2,1)S(1)}, bf16[256,1024]{1,0:T(8,128)(2,1)S(1)}, u32[]{:S(2)}, u32[]{:S(2)}) collective-permute-start(bf16[256,1024]{1,0:T(8,128)(2,1)S(1)} %slice_bitcast_fusion.2), channel_id=1, source_target_pairs={{0,1},{1,0},{2,3},{3,2},{4,5},{5,4},{6,7},{7,6},{8,9},{9,8},{10,11... | collective-permute-start | bytes 1572872 | tf_op jit(solution)/shard_map/ppermute | solution.py:28
  546.6 27.7 %collective-permute-start.82 = (bf16[256,1024]{1,0:T(8,128)(2,1)S(1)}, bf16[256,1024]{1,0:T(8,128)(2,1)S(1)}, u32[]{:S(2)}, u32[]{:S(2)}) collective-permute-start(bf16[256,1024]{1,0:T(8,128)(2,1)S(1)} %slice_bitcast_fusion), channel_id=1, source_target_pairs={{0,1},{1,0},{2,3},{3,2},{4,5},{5,4},{6,7},{7,6},{8,9},{9,8},{10,11... | collective-permute-start | bytes 1572872 | tf_op jit(solution)/shard_map/ppermute | solution.py:28
  (81 other events, 1684.7 us)

commit v2 on v1

v2 whole, which is shorter than its diff:
```python
import functools

import jax
import jax.numpy as jnp
from jax import lax
from jax.experimental import pallas as pl
from jax.experimental.pallas import tpu as pltpu
from jax.sharding import PartitionSpec as P

HEAD_SIZE = 128
QUERY_HEADS = 32
KEY_VALUE_HEADS = 4
ROPE_BASE = 1000000.0
CORE, Y, NEAR = 1, 2, 4
GROUP = (0, CORE, NEAR, NEAR | CORE)
VMEM_LIMIT = 48 * 1024 * 1024
LOG2E = 1.4426950408889634
VM = pl.BlockSpec(memory_space=pltpu.VMEM)
SM = pl.BlockSpec(memory_space=pltpu.SMEM)


def swap(x, mask):
    n = lax.axis_size("ctx")
    return lax.ppermute(x, "ctx", [(i, i ^ mask) for i in range(n)])


def swap_rep(x, mask):
    n = lax.axis_size("rep")
    return lax.ppermute(x, "rep", [(i, i ^ mask) for i in range(n)])


def after(x, *tokens):
    tokens = tuple(t for t in tokens if t is not None)
    if not tokens:
        return x
    return lax.optimization_barrier((x,) + tokens)[0]


def gather_rep(x, axis):
    rep = lax.axis_index("rep")
    bit = 1
    while bit < lax.axis_size("rep"):
        other = swap_rep(x, bit)
        high = (rep & bit) != 0
        x = jnp.concatenate([jnp.where(high, other, x), jnp.where(high, x, other)], axis=axis)
        bit *= 2
    return x


def call(body, out_shape, specs, flops, nbytes, args, scratch=(), name=None):
    outs = tuple(out_shape)
    return pl.pallas_call(
        body,
        out_shape=outs,
        in_specs=specs,
        out_specs=tuple(VM for _ in outs),
        scratch_shapes=list(scratch),
        compiler_params=pltpu.CompilerParams(vmem_limit_bytes=VMEM_LIMIT),
        cost_estimate=pl.CostEstimate(flops=flops, bytes_accessed=nbytes, transcendentals=0),
        name=name,
    )(*args)


def norm_body(masks, place, tokens, gain, own, core, far):
    ctx, rep = place[0], place[1]
    rows, width = tokens.shape
    kb = own.shape[1] // len(masks)
    step = 32
    share = far.shape[0]

    def normed(part, out_part, targets):
        t = tokens[part, :].astype(jnp.float32)
        scale = lax.rsqrt(jnp.sum(t * t, axis=-1, keepdims=True) * (1.0 / width) + 1e-06)
        for e, ref, first in targets:
            for j, m in enumerate(masks):
                block = pl.ds(pl.multiple_of((ctx ^ (m | e)) * kb, 128), kb)
                v = tokens[part, block].astype(jnp.float32) * scale * gain[:, block].astype(jnp.float32)
                ref[out_part, first + j * kb : first + (j + 1) * kb] = v.astype(jnp.bfloat16)

    def distant(i, carry):
        part = pl.ds(pl.multiple_of(rep * share + i * step, step), step)
        normed(part, pl.ds(i * step, step), ((NEAR, far, 0), (NEAR | CORE, far, own.shape[1])))
        return carry

    def local(i, carry):
        part = pl.ds(i * step, step)
        normed(part, part, ((0, own, 0), (CORE, core, 0)))
        return carry

    lax.fori_loop(0, share // step, distant, 0)
    lax.fori_loop(0, rows // step, local, 0)


def times(a, weights, columns):
    kb = weights[0].shape[0]
    total = None
    for j, w in enumerate(weights):
        part = jnp.dot(a[:, j * kb : (j + 1) * kb], w[:, columns], preferred_element_type=jnp.float32)
        total = part if total is None else total + part
    return total


def kv_body(a0, a1, a4, a5, *refs):
    weights, (kept, sent) = refs[:-2], refs[-2:]
    rows = a0.shape[0]
    for out, parts in ((kept, (a0, a4)), (sent, (a1, a5))):
        for i, a in enumerate(parts):
            out[i * rows : (i + 1) * rows, :] = times(a, weights, slice(None)).astype(out.dtype)


def query_body(place, a0, a1, a4, a5, *refs):
    weights, (kept, sent) = refs[:-2], refs[-2:]
    core = place[0] & 1
    rows, half = a0.shape[0], kept.shape[1]
    for i, a in enumerate((a0, a1, a4, a5)):
        mine = pl.ds(pl.multiple_of(core * half, 128), half)
        other = pl.ds(pl.multiple_of((1 - core) * half, 128), half)
        kept[i * rows : (i + 1) * rows, :] = times(a, weights, mine)
        turned = i ^ 1
        sent[turned * rows : (turned + 1) * rows, :] = times(a, weights, other).astype(jnp.bfloat16)


def halve_body(place, kept, came, mine, sent):
    near = (place[0] >> 2) & 1
    n = mine.shape[1]
    half = mine.shape[0] // 2
    here = pl.ds(pl.multiple_of(near * n, 128), n)
    there = pl.ds(pl.multiple_of((1 - near) * n, 128), n)
    mine[...] = kept[:, here] + came[:, here].astype(jnp.float32)
    for i in range(2):
        rows, turned = slice(i * half, (i + 1) * half), slice((1 - i) * half, (2 - i) * half)
        sent[turned, :] = (kept[rows, there] + came[rows, there].astype(jnp.float32)).astype(jnp.bfloat16)


def rotate(v, cosine, sine):
    half = HEAD_SIZE // 2
    turned = jnp.concatenate([v[:, half:], v[:, :half]], axis=1)
    return v * cosine + turned * sine


def attend_body(n_bits, place, mine, other, bias, cosine, sine, cache, out, q, acc, top):
    ctx = place[0]
    rows4, width = mine.shape
    rows = rows4 // 4
    pair = 2 * rows
    heads = width // HEAD_SIZE
    tile = heads * pair
    for h in range(heads):
        cols = slice(h * HEAD_SIZE, (h + 1) * HEAD_SIZE)
        v = mine[:, cols] + other[:, cols].astype(jnp.float32) + bias[:, cols].astype(jnp.float32)
        v = rotate(v, cosine[...], sine[...]).astype(jnp.bfloat16)
        for f in range(2):
            q[f * tile + h * pair : f * tile + (h + 1) * pair, :] = v[f * pair : (f + 1) * pair, :]
    factor = LOG2E * HEAD_SIZE ** (-0.5)
    ones = jnp.ones((pair, HEAD_SIZE), jnp.bfloat16)

    def place_of(k):
        return (k >> 2) | ((k & 2) << (n_bits - 3)) | ((k & 1) << (n_bits - 1))

    def load(k, first):
        spots = [pl.ds(pl.multiple_of(place_of(b) * rows, 128), rows) for b in (k, k ^ 1)]
        return jnp.concatenate([cache[s, first : first + HEAD_SIZE] for s in spots], axis=0)

    def scores(part, k):
        return lax.dot_general(
            q[part, :], load(k, 0), (((1,), (1,)), ((), ())), preferred_element_type=jnp.float32
        )

    def weighted(s, m, k):
        p = jnp.exp2((s - jnp.concatenate([m] * (pair // HEAD_SIZE), axis=1)) * factor).astype(jnp.bfloat16)
        return jnp.dot(p, jnp.concatenate([load(k, HEAD_SIZE), ones], axis=1), preferred_element_type=jnp.float32)

    def begin(f):
        part = slice(f * tile, (f + 1) * tile)
        s = scores(part, NEAR * f)
        r = lax.broadcasted_iota(jnp.int32, s.shape, 0) % pair
        c = lax.broadcasted_iota(jnp.int32, s.shape, 1)
        odd = ctx & 1
        row = ((r // rows) ^ odd) * rows + r % rows
        col = ((c // rows) ^ odd) * rows + c % rows
        s = jnp.where(col <= row, s, -1e30)
        m = jnp.broadcast_to(jnp.max(s, axis=-1, keepdims=True), (tile, HEAD_SIZE))
        top[part, :] = m
        acc[part, :] = weighted(s, m, NEAR * f)

    def step(start, k):
        part = pl.ds(start, tile)
        s = scores(part, k)
        old = top[part, :]
        m = jnp.maximum(old, jnp.max(s, axis=-1, keepdims=True))
        top[part, :] = m
        shrink = jnp.exp2((old - m) * factor)
        acc[part, :] = acc[part, :] * jnp.concatenate([shrink, shrink], axis=1) + weighted(s, m, k)

    begin(0)
    begin(1)
    here, there = ctx >> 1, (ctx ^ NEAR) >> 1
    common = jnp.minimum(here, there)

    def both(b, carry):
        k = ctx ^ (2 * b)
        step(0, k)
        step(tile, k)
        return carry

    def single(b, carry):
        step(pl.multiple_of(jnp.where(here > there, 0, tile), 128), ctx ^ (2 * b))
        return carry

    lax.fori_loop(0, common, both, 0)
    lax.fori_loop(common, jnp.maximum(here, there), single, 0)
    for f in range(2):
        for h in range(heads):
            a = acc[f * tile + h * pair : f * tile + (h + 1) * pair, :]
            part = (a[:, :HEAD_SIZE] / a[:, HEAD_SIZE:]).astype(jnp.bfloat16)
            out[f * pair : (f + 1) * pair, h * HEAD_SIZE : (h + 1) * HEAD_SIZE] = part


def collect_body(n_parts, heads_each, place, *refs):
    pieces, out = refs[:-1], refs[-1]
    ctx, rep = place[0], place[1]
    rows = pieces[0].shape[0] // 4
    wide = pieces[0].shape[1]
    members = out.shape[0]
    size = rows // members
    for d, distance in enumerate(GROUP):
        owner = ctx ^ distance
        group = ((owner >> 2) & 1) * 2 + (owner & 1)
        for i in range(n_parts):
            piece = pieces[d * n_parts + i]
            column = pl.ds(pl.multiple_of(group * (n_parts * wide) + i * wide, 128), wide)
            for far in range(members):
                for e in range(4):
                    part = pl.ds(pl.multiple_of((e ^ d) * rows + (rep ^ far) * size, size), size)
                    out[far, e * size : (e + 1) * size, column] = piece[part, :]


def output_body(att, *refs):
    weights, out = refs[:-1], refs[-1]
    n = weights[0].shape[1]
    for far in range(att.shape[0]):
        for j, w in enumerate(weights):
            out[far, :, j * n : (j + 1) * n] = jnp.dot(
                att[far], w[...], preferred_element_type=jnp.float32
            ).astype(jnp.bfloat16)


def place_body(masks, n_sub, place, *refs):
    sums, fars, cores, out = refs[:n_sub], refs[n_sub : 2 * n_sub], refs[2 * n_sub : -1], refs[-1]
    ctx = place[0]
    size = out.shape[0]
    sub = sums[0].shape[1] // len(masks)
    for s in range(n_sub):
        sources = ((0, sums[s], 0), (NEAR, fars[s], 0), (CORE, cores[s], 0), (NEAR | CORE, cores[s], size))
        for e, ref, first in sources:
            for j, m in enumerate(masks):
                start = (ctx ^ (m | e)) * (sub * n_sub) + s * sub
                out[:, pl.ds(pl.multiple_of(start, 128), sub)] = ref[first : first + size, j * sub : (j + 1) * sub]


class Stream:
    def __init__(self, depth):
        self.depth, self.done = depth, []

    def swap(self, x, mask):
        if len(self.done) >= self.depth:
            x = after(x, self.done[-self.depth])
        got = swap(x, mask)
        self.done.append(got)
        return got


def per_device(tokens, norm_gain, q_weight, q_bias, kv_weight, kv_bias, out_weight):
    rows, width = tokens.shape
    n_ctx, n_rep = lax.axis_size("ctx"), lax.axis_size("rep")
    n_bits = n_ctx.bit_length() - 1
    ctx, rep = lax.axis_index("ctx"), lax.axis_index("rep")
    place = jnp.stack([ctx, rep]).astype(jnp.int32)
    head_group = QUERY_HEADS // KEY_VALUE_HEADS
    local_heads = q_weight.shape[1] // HEAD_SIZE
    own_heads = local_heads // 4
    high_bits = [1 << b for b in range(3, n_bits)]
    masks = [0]
    for bit in high_bits + [Y]:
        masks = masks + [m | bit for m in masks]
    masks = sorted(masks)
    n_masks = len(masks)

    n_q = min(4, own_heads)
    heads = own_heads // n_q
    n = heads * HEAD_SIZE
    groups = q_weight.reshape(q_weight.shape[0], 2, 2, n_q, n)
    groups = jnp.swapaxes(groups, 1, 2)
    bias = q_bias.reshape(4, n_q, n)
    n_out = max(1, min(4, out_weight.shape[1] // 128))
    out_cols = out_weight.shape[1] // n_out
    pieces = {"kv": kv_weight}
    for i in range(n_q):
        pieces[f"q{i}"] = groups[:, :, :, i].reshape(q_weight.shape[0], 4 * n)
    for i in range(n_out):
        pieces[f"o{i}"] = out_weight[:, i * out_cols : (i + 1) * out_cols]
    blocks = {name: {0: piece} for name, piece in pieces.items()}
    z_stream, y_stream = Stream(2), Stream(2)

    def high(name):
        if name in blocks:
            for bit in high_bits:
                for m in list(blocks[name]):
                    blocks[name][m | bit] = z_stream.swap(blocks[name][m], bit)

    def first(name):
        if name in blocks:
            blocks[name][Y] = y_stream.swap(blocks[name][0], Y)

    def rest(name):
        if name in blocks:
            for m in sorted(blocks[name]):
                if m and not m & Y:
                    blocks[name][m | Y] = y_stream.swap(blocks[name][m], Y)

    def weights(name):
        return [blocks[name][m] for m in masks]

    high("kv")
    first("kv")
    high("q0")
    first("q0")
    rest("kv")

    kw = width // 4
    a_own, a_core, a_far = call(
        functools.partial(norm_body, masks),
        (
            jax.ShapeDtypeStruct((rows, kw), jnp.bfloat16),
            jax.ShapeDtypeStruct((rows, kw), jnp.bfloat16),
            jax.ShapeDtypeStruct((rows // n_rep, 2 * kw), jnp.bfloat16),
        ),
        [SM, VM, VM], 0, 3 * rows * width * 2, (place, tokens, norm_gain.reshape(1, width)), name="normed",
    )
    a_1 = swap(a_core, CORE)
    a_via = gather_rep(swap(a_far[:, kw:], NEAR), 0)
    a_4 = gather_rep(swap(a_far[:, :kw], NEAR), 0)
    a_5 = swap(a_via, CORE)
    shares = (a_own, a_1, a_4, a_5)

    high("q1")
    first("q1")
    rest("q0")
    high("q2")
    first("q2")
    rest("q1")

    middle = HEAD_SIZE // 2
    exponent = jnp.arange(middle, dtype=jnp.float32) * (2.0 / HEAD_SIZE)
    starts = jnp.stack([(ctx ^ e) * rows for e in GROUP])
    positions = (starts[:, None] + jnp.arange(rows, dtype=jnp.int32)[None, :]).reshape(-1).astype(jnp.float32)
    angles = positions[:, None] * (ROPE_BASE ** (-exponent))[None, :]
    cosine, sine = jnp.cos(angles), jnp.sin(angles)
    cosine = jnp.concatenate([cosine, cosine], axis=1)
    sine = jnp.concatenate([-sine, sine], axis=1)

    kv_cols = kv_weight.shape[1]
    kept, sent = call(
        kv_body,
        (
            jax.ShapeDtypeStruct((2 * rows, kv_cols), jnp.float32),
            jax.ShapeDtypeStruct((2 * rows, kv_cols), jnp.bfloat16),
        ),
        [VM] * (4 + n_masks), 8 * rows * kw * kv_cols, 2 * kw * (4 * rows + kv_cols),
        (*shares, *weights("kv")), name="kv_project",
    )
    total = kept + swap(sent, CORE).astype(jnp.float32)
    total = total[:rows] + swap(total[rows:].astype(jnp.bfloat16), NEAR).astype(jnp.float32)
    total = total + kv_bias.astype(jnp.float32)
    n_blocks = kv_cols // HEAD_SIZE
    columns = []
    for b in range(n_blocks):
        v = total[:, b * HEAD_SIZE : (b + 1) * HEAD_SIZE]
        columns.append(jnp.where(rep * n_blocks + b < KEY_VALUE_HEADS, rotate(v, cosine[:rows], sine[:rows]), v))
    kv_local = jnp.concatenate(columns, axis=1).astype(jnp.bfloat16)
    key_value_cache = gather_rep(kv_local, 1)

    def used(near):
        head = (rep * local_heads + near * (local_heads // 2)) // head_group
        parts = [
            lax.dynamic_slice_in_dim(key_value_cache, (offset + head) * HEAD_SIZE, HEAD_SIZE, 1)
            for offset in (0, KEY_VALUE_HEADS)
        ]
        return jnp.concatenate(parts, axis=1)

    near = (ctx >> 2) & 1
    cache = jnp.concatenate([used(near), swap(used(1 - near), NEAR)], axis=0)
    for bit in high_bits:
        cache = jnp.concatenate([cache, z_stream.swap(cache, bit)], axis=0)
    high("q3")
    first("q3")
    rest("q2")
    first("o0")
    cache = jnp.concatenate([cache, y_stream.swap(cache, Y)], axis=0)
    cache = jnp.concatenate([cache, swap(cache, CORE)], axis=0)
    rest("q3")
    for i in range(n_out):
        high(f"o{i}")
        first(f"o{i + 1}")
        rest(f"o{i}")

    n_tokens = rows * n_ctx
    own_bias = lax.dynamic_index_in_dim(bias, near * 2 + (ctx & 1), 0, keepdims=False)
    att = {d: [] for d in GROUP}
    for i in range(n_q):
        kept, sent = call(
            query_body,
            (
                jax.ShapeDtypeStruct((4 * rows, 2 * n), jnp.float32),
                jax.ShapeDtypeStruct((4 * rows, 2 * n), jnp.bfloat16),
            ),
            [SM] + [VM] * (4 + n_masks), 8 * rows * kw * 4 * n, 2 * kw * (4 * rows + 4 * n),
            (place, *shares, *weights(f"q{i}")), name=f"q_project{i}",
        )
        mine, sent = call(
            halve_body,
            (jax.ShapeDtypeStruct((4 * rows, n), jnp.float32), jax.ShapeDtypeStruct((4 * rows, n), jnp.bfloat16)),
            [SM, VM, VM], 0, 4 * rows * n * 18, (place, kept, swap(sent, CORE)), name=f"q_halve{i}",
        )
        (attended,) = call(
            functools.partial(attend_body, n_bits),
            (jax.ShapeDtypeStruct((4 * rows, n), jnp.bfloat16),),
            [SM] + [VM] * 6, 4 * heads * 4 * rows * n_tokens * HEAD_SIZE * 2, 2 * n_tokens * HEAD_SIZE * 2,
            (place, mine, swap(sent, NEAR), own_bias[i : i + 1], cosine, sine, cache),
            scratch=[
                pltpu.VMEM((4 * heads * rows, HEAD_SIZE), jnp.bfloat16),
                pltpu.VMEM((4 * heads * rows, 2 * HEAD_SIZE), jnp.float32),
                pltpu.VMEM((4 * heads * rows, HEAD_SIZE), jnp.float32),
            ],
            name=f"attend{i}",
        )
        far = swap(attended, NEAR)
        att[0].append(attended)
        att[NEAR].append(far)
        att[CORE].append(swap(attended, CORE))
        att[NEAR | CORE].append(swap(far, CORE))
    size = rows // n_rep
    (collected,) = call(
        functools.partial(collect_body, n_q, heads),
        (jax.ShapeDtypeStruct((n_rep, 4 * size, local_heads * HEAD_SIZE), jnp.bfloat16),),
        [SM] + [VM] * (4 * n_q), 0, 16 * rows * local_heads * HEAD_SIZE,
        (place, *[a for d in GROUP for a in att[d]]), name="collected",
    )

    sums, fars, cores = [], [], []
    for s in range(n_out):
        cols = out_cols * n_masks
        (partial,) = call(
            output_body,
            (jax.ShapeDtypeStruct((n_rep, 4 * size, cols), jnp.bfloat16),),
            [VM] * (1 + n_masks), 8 * rows * out_weight.shape[0] * cols,
            2 * out_weight.shape[0] * (4 * rows + cols) + 8 * rows * cols,
            (collected, *weights(f"o{s}")), name=f"out_project{s}",
        )
        total = partial[0].astype(jnp.float32)
        for far in range(1, n_rep):
            total = total + swap_rep(partial[far], far).astype(jnp.float32)
        total = total.astype(jnp.bfloat16)
        came = swap(total[2 * size :], NEAR)
        sums.append(total)
        fars.append(came)
        cores.append(swap(jnp.concatenate([total[size : 2 * size], came[size:]], axis=0), CORE))
    (result,) = call(
        functools.partial(place_body, masks, n_out),
        (jax.ShapeDtypeStruct((size, width), jnp.bfloat16),),
        [SM] + [VM] * (3 * n_out), 0, 2 * size * width * 2, (place, *sums, *fars, *cores), name="placed",
    )
    return result, key_value_cache


def solution(mesh):
    in_specs = (
        P("ctx", None),
        P(),
        P("ctx", "rep"),
        P("rep"),
        P("ctx", "rep"),
        P("rep"),
        P("rep", "ctx"),
    )
    out_specs = (P(("ctx", "rep"), None), P("ctx", None))
    return jax.shard_map(per_device, mesh=mesh, in_specs=in_specs, out_specs=out_specs, check_vma=False)
```

time: 611 us -> 408 us (0.67)
  Pallas kernels: 233 us -> 99.6 us
  waiting for transfers between devices: 280 us -> 204 us
  local copies, waits for them, and re-layouts: 17.9 us -> 27.7 us
  starting transfers between devices: 57.4 us -> 48.4 us
  other arithmetic: 11.4 us -> 19.2 us
    pallas_call x15 -> x20, Pallas kernels: 233 us -> 99.6 us  [call(): pl.pallas_call(body, out_shape=outs, in_specs=specs, out_specs=tuple((VM...]
    ppermute x81 -> x65, waiting for transfers between devices: 242 us -> 174 us  [swap(): return lax.ppermute(x, 'ctx', [(i, i ^ mask) for i in range(n)])]
    ppermute x81 -> x65, starting transfers between devices: 50.5 us -> 40.6 us  [swap(): return lax.ppermute(x, 'ctx', [(i, i ^ mask) for i in range(n)])]
    ppermute x6 -> x7, waiting for transfers between devices: 38.9 us -> 30.6 us  [swap_rep(): return lax.ppermute(x, 'rep', [(i, i ^ mask) for i in range(n)])]
    reshape x4 -> x2, local copies, waits for them, and re-layouts: 0.02 us -> 7.72 us  [per_device(): groups = q_weight.reshape(q_weight.shape[0], 2, 2, n_q, n)]
  transfers between devices with their start and end apart: 87 -> 72, of which waited for: 28 -> 28; matrix products, arithmetic and copies ran while one was open for 4% -> 10% of each run, Pallas kernels for 37% -> 22%
where the time goes in v2:
time: 408 us; the launch traced here: 401 us
  waiting for transfers between devices  204 us (50%)
  Pallas kernels  99.6 us (24%)
  starting transfers between devices  48.4 us (12%)
  local copies, waits for them, and re-layouts  27.7 us (7%)
  other arithmetic  19.2 us (5%)
    ppermute x65, waiting for transfers between devices, swap(): return lax.ppermute(x, 'ctx', [(i, i ^ mask) for i in range(n)])  174 us
    pallas_call x20, Pallas kernels, call(): pl.pallas_call(body, out_shape=outs, in_specs=specs, out_specs=tuple((VM...  99.6 us
    ppermute x65, starting transfers between devices, swap(): return lax.ppermute(x, 'ctx', [(i, i ^ mask) for i in range(n)])  40.6 us
    ppermute x7, waiting for transfers between devices, swap_rep(): return lax.ppermute(x, 'rep', [(i, i ^ mask) for i in range(n)])  30.6 us
    unnamed x92, local copies, waits for them, and re-layouts  8.29 us
  transfers between devices with their start and end apart: 72, of which 28 were waited for; matrix products, arithmetic and copies ran while one was open for 10% of the time, Pallas kernels for 22%

profile of v2, /device:TPU:28, one launch (start us, length us, event | category | flops | bytes accessed | tf_op | source)
XLA Modules:
  0.0 401.2 jit_solution(9879013790207703021)
XLA Ops:
  1.5 5.0 %normed.1 = (bf16[256,2048]{1,0:T(8,128)(2,1)S(1)}, bf16[256,2048]{1,0:T(8,128)(2,1)S(1)}, bf16[128,4096]{1,0:T(8,128)(2,1)S(1)}) custom-call(s32[2]{0:T(128)S(1)} %pad_add_fusion.place, bf16[256,8192]{1,0:T(8,128)(2,1)} %tokens.1, bf16[1,8192]{1,0:T(2,128)(2,1)S(1)} %reshape.48.gain), custom_call_target="tpu_custom_call" | custom-call | bytes 12582912 | tf_op jit(solution)/shard_map/normed/pallas_call | solution.py:52
  8.7 12.9 %collective-permute-done.3 = bf16[128,2048]{1,0:T(8,128)(2,1)} collective-permute-done((bf16[128,2048]{1,0:T(8,128)(2,1)S(1)}, bf16[128,2048]{1,0:T(8,128)(2,1)}, u32[]{:S(2)}, u32[]{:S(2)}) %collective-permute-start.3) | collective-permute-done | bytes 524320 | tf_op jit(solution)/shard_map/ppermute | solution.py:24
  23.0 8.6 %collective-permute-done.1 = bf16[128,2048]{1,0:T(8,128)(2,1)} collective-permute-done((bf16[128,2048]{1,0:T(8,128)(2,1)S(1)}, bf16[128,2048]{1,0:T(8,128)(2,1)}, u32[]{:S(2)}, u32[]{:S(2)}) %collective-permute-start.1) | collective-permute-done | bytes 524320 | tf_op jit(solution)/shard_map/ppermute | solution.py:24
  34.0 10.8 %collective-permute-done.2 = bf16[128,2048]{1,0:T(8,128)(2,1)} collective-permute-done((bf16[128,2048]{1,0:T(8,128)(2,1)}, bf16[128,2048]{1,0:T(8,128)(2,1)}, u32[]{:S(2)}, u32[]{:S(2)}) %collective-permute-start.2) | collective-permute-done | bytes 524320 | tf_op jit(solution)/shard_map/ppermute | solution.py:29
  44.8 2.6 broadcast_select_fusion.1
  48.5 9.5 %collective-permute-done.8.refs_2_ = bf16[512,512]{1,0:T(8,128)(2,1)} collective-permute-done((bf16[512,512]{1,0:T(8,128)(2,1)}, bf16[512,512]{1,0:T(8,128)(2,1)}, u32[]{:S(2)}, u32[]{:S(2)}) %collective-permute-start.8) | collective-permute-done | bytes 524320 | tf_op jit(solution)/shard_map/ppermute | solution.py:24
  58.5 4.4 %reshape.49 = bf16[512,2,2,4,128]{4,3,2,1,0:T(4,128)(2,1)} reshape(bf16[512,2048]{1,0:T(8,128)(2,1)} %param.9) | data formatting | bytes 4194304 | tf_op jit(solution)/shard_map/reshape | solution.py:292
  62.9 3.3 copy.12
  67.3 4.8 %collective-permute-done.10.refs_3_ = bf16[512,512]{1,0:T(8,128)(2,1)} collective-permute-done((bf16[512,512]{1,0:T(8,128)(2,1)}, bf16[512,512]{1,0:T(8,128)(2,1)}, u32[]{:S(2)}, u32[]{:S(2)}) %collective-permute-start.10) | collective-permute-done | bytes 524320 | tf_op jit(solution)/shard_map/ppermute | solution.py:24
  72.2 5.4 %kv_project.1 = (f32[512,512]{1,0:T(8,128)S(1)}, bf16[512,512]{1,0:T(8,128)(2,1)}) custom-call(bf16[256,2048]{1,0:T(8,128)(2,1)S(1)} %get-tuple-element.48.a0, bf16[256,2048]{1,0:T(8,128)(2,1)S(1)} %collective-permute-done.a1, bf16[256,2048]{1,0:T(8,128)(2,1)} %pad_maximum_fusion.a4, bf16[256,2048]{1,0:T(8,128)(2,1)} %collective-permute-done.5.a5, ...), custom_call_target="tpu_custom_call" | custom-call | flops 2147483648 | bytes 6291456 | tf_op jit(solution)/shard_map/kv_project/pallas_call | solution.py:52
  77.5 2.4 fusion.27
  85.5 3.0 collective-permute-start.18
  88.4 6.1 %collective-permute-done.6.refs_1_ = bf16[512,512]{1,0:T(8,128)(2,1)S(1)} collective-permute-done((bf16[512,512]{1,0:T(8,128)(2,1)S(1)}, bf16[512,512]{1,0:T(8,128)(2,1)S(1)}, u32[]{:S(2)}, u32[]{:S(2)}) %collective-permute-start.6) | collective-permute-done | bytes 524320 | tf_op jit(solution)/shard_map/ppermute | solution.py:24
  95.0 19.8 %collective-permute-done.7.refs_2_ = bf16[512,512]{1,0:T(8,128)(2,1)S(1)} collective-permute-done((bf16[512,512]{1,0:T(8,128)(2,1)S(1)}, bf16[512,512]{1,0:T(8,128)(2,1)S(1)}, u32[]{:S(2)}, u32[]{:S(2)}) %collective-permute-start.7) | collective-permute-done | bytes 524320 | tf_op jit(solution)/shard_map/ppermute | solution.py:24
  120.6 16.8 %collective-permute-done.18.refs_2_ = bf16[512,512]{1,0:T(8,128)(2,1)} collective-permute-done((bf16[512,512]{1,0:T(8,128)(2,1)S(1)}, bf16[512,512]{1,0:T(8,128)(2,1)}, u32[]{:S(2)}, u32[]{:S(2)}) %collective-permute-start.18) | collective-permute-done | bytes 524320 | tf_op jit(solution)/shard_map/ppermute | solution.py:24
  143.7 4.9 %collective-permute-done.20.refs_2_ = bf16[512,512]{1,0:T(8,128)(2,1)} collective-permute-done((bf16[512,512]{1,0:T(8,128)(2,1)S(1)}, bf16[512,512]{1,0:T(8,128)(2,1)}, u32[]{:S(2)}, u32[]{:S(2)}) %collective-permute-start.20) | collective-permute-done | bytes 524320 | tf_op jit(solution)/shard_map/ppermute | solution.py:24
  148.6 3.7 collective-permute-done.21.refs_3_
  155.7 2.7 fusion.26
  158.5 2.9 collective-permute-start.32
  161.4 2.2 collective-permute-done.31.refs_1_
  166.0 13.9 %collective-permute-done.19 = bf16[512,256]{1,0:T(8,128)(2,1)S(1)} collective-permute-done((bf16[512,256]{1,0:T(8,128)(2,1)S(1)}, bf16[512,256]{1,0:T(8,128)(2,1)S(1)}, u32[]{:S(2)}, u32[]{:S(2)}) %collective-permute-start.19) | collective-permute-done | bytes 262176 | tf_op jit(solution)/shard_map/ppermute | solution.py:24
  186.7 4.1 %q_project0.1 = (f32[1024,256]{1,0:T(8,128)S(1)}, bf16[1024,256]{1,0:T(8,128)(2,1)S(1)}) custom-call(s32[2]{0:T(128)S(1)} %pad_add_fusion.place, bf16[256,2048]{1,0:T(8,128)(2,1)S(1)} %copy-done.6, bf16[256,2048]{1,0:T(8,128)(2,1)S(1)} %copy-done.9, bf16[256,2048]{1,0:T(8,128)(2,1)} %pad_maximum_fusion.a4, bf16[256,2048]{1,0:T(8,128)(2,1)} %collective-permute-done.5.a5, ...), custom_call_target="tpu_custom_call" | custom-call | flops 2147483648 | bytes 6291456 | tf_op jit(solution)/shard_map/q_project0/pallas_call | solution.py:52
  190.9 11.5 %collective-permute-done.32.refs_2_ = bf16[512,512]{1,0:T(8,128)(2,1)} collective-permute-done((bf16[512,512]{1,0:T(8,128)(2,1)S(1)}, bf16[512,512]{1,0:T(8,128)(2,1)}, u32[]{:S(2)}, u32[]{:S(2)}) %collective-permute-start.32) | collective-permute-done | bytes 524320 | tf_op jit(solution)/shard_map/ppermute | solution.py:24
  204.6 4.1 %q_project1.1 = (f32[1024,256]{1,0:T(8,128)S(1)}, bf16[1024,256]{1,0:T(8,128)(2,1)S(1)}) custom-call(s32[2]{0:T(128)S(1)} %pad_add_fusion.place, bf16[256,2048]{1,0:T(8,128)(2,1)S(1)} %copy-done.6, bf16[256,2048]{1,0:T(8,128)(2,1)S(1)} %copy-done.9, bf16[256,2048]{1,0:T(8,128)(2,1)} %pad_maximum_fusion.a4, bf16[256,2048]{1,0:T(8,128)(2,1)} %collective-permute-done.5.a5, ...), custom_call_target="tpu_custom_call" | custom-call | flops 2147483648 | bytes 6291456 | tf_op jit(solution)/shard_map/q_project1/pallas_call | solution.py:52
  208.8 4.1 %q_project2.1 = (f32[1024,256]{1,0:T(8,128)S(1)}, bf16[1024,256]{1,0:T(8,128)(2,1)S(1)}) custom-call(s32[2]{0:T(128)S(1)} %pad_add_fusion.place, bf16[256,2048]{1,0:T(8,128)(2,1)S(1)} %copy-done.6, bf16[256,2048]{1,0:T(8,128)(2,1)S(1)} %copy-done.9, bf16[256,2048]{1,0:T(8,128)(2,1)} %pad_maximum_fusion.a4, bf16[256,2048]{1,0:T(8,128)(2,1)} %collective-permute-done.5.a5, ...), custom_call_target="tpu_custom_call" | custom-call | flops 2147483648 | bytes 6291456 | tf_op jit(solution)/shard_map/q_project2/pallas_call | solution.py:52
  217.6 7.7 %collective-permute-done.52.refs_1_ = bf16[2048,128]{1,0:T(8,128)(2,1)S(1)} collective-permute-done((bf16[2048,128]{1,0:T(8,128)(2,1)S(1)}, bf16[2048,128]{1,0:T(8,128)(2,1)S(1)}, u32[]{:S(2)}, u32[]{:S(2)}) %collective-permute-start.52) | collective-permute-done | bytes 524320 | tf_op jit(solution)/shard_map/ppermute | solution.py:24
  225.3 4.9 %q_project3.1 = (f32[1024,256]{1,0:T(8,128)S(1)}, bf16[1024,256]{1,0:T(8,128)(2,1)}) custom-call(s32[2]{0:T(128)S(1)} %pad_add_fusion.place, bf16[256,2048]{1,0:T(8,128)(2,1)S(1)} %copy-done.7, bf16[256,2048]{1,0:T(8,128)(2,1)S(1)} %copy-done.10, bf16[256,2048]{1,0:T(8,128)(2,1)} %pad_maximum_fusion.a4, bf16[256,2048]{1,0:T(8,128)(2,1)} %collective-permute-done.5.a5, ...), custom_call_target="tpu_custom_call" | custom-call | flops 2147483648 | bytes 6291456 | tf_op jit(solution)/shard_map/q_project3/pallas_call | solution.py:52
  230.2 8.0 %collective-permute-done.53.refs_2_ = bf16[2048,128]{1,0:T(8,128)(2,1)S(1)} collective-permute-done((bf16[2048,128]{1,0:T(8,128)(2,1)S(1)}, bf16[2048,128]{1,0:T(8,128)(2,1)S(1)}, u32[]{:S(2)}, u32[]{:S(2)}) %collective-permute-start.53) | collective-permute-done | bytes 524320 | tf_op jit(solution)/shard_map/ppermute | solution.py:24
  244.3 3.2 collective-permute-start.13
  249.3 3.8 collective-permute-done.50.refs_3_
  253.0 10.8 %collective-permute-done.56.refs_1_ = bf16[2048,128]{1,0:T(8,128)(2,1)S(1)} collective-permute-done((bf16[2048,128]{1,0:T(8,128)(2,1)S(1)}, bf16[2048,128]{1,0:T(8,128)(2,1)S(1)}, u32[]{:S(2)}, u32[]{:S(2)}) %collective-permute-start.56) | collective-permute-done | bytes 524320 | tf_op jit(solution)/shard_map/ppermute | solution.py:24
  263.8 2.5 collective-permute-done.57.refs_2_
  269.7 9.0 %attend0.1.refs_0_ = bf16[1024,128]{1,0:T(8,128)(2,1)S(1)} custom-call(s32[2]{0:T(128)S(1)} %pad_add_fusion.place, f32[1024,128]{1,0:T(8,128)S(1)} %get-tuple-element.55.mine, bf16[1024,128]{1,0:T(8,128)(2,1)S(1)} %collective-permute-done.13.other, bf16[1,128]{1,0:T(2,128)(2,1)S(1)} %get-tuple-element.134.bias, f32[1024,128]{1,0:T(8,128)S(1)} %get-tuple-element.137.cosine, ...), custom_call_target="tpu_custom_call" | custom-call | flops 4294967296 | bytes 2097152 | tf_op jit(solution)/shard_map/attend0/pallas_call | solution.py:52
  278.8 9.0 %attend1.1.refs_1_ = bf16[1024,128]{1,0:T(8,128)(2,1)S(1)} custom-call(s32[2]{0:T(128)S(1)} %pad_add_fusion.place, f32[1024,128]{1,0:T(8,128)S(1)} %get-tuple-element.68.mine, bf16[1024,128]{1,0:T(8,128)(2,1)S(1)} %collective-permute-done.27.other, bf16[1,128]{1,0:T(2,128)(2,1)S(1)} %get-tuple-element.133.bias, f32[1024,128]{1,0:T(8,128)S(1)} %get-tuple-element.137.cosine, ...), custom_call_target="tpu_custom_call" | custom-call | flops 4294967296 | bytes 2097152 | tf_op jit(solution)/shard_map/attend1/pallas_call | solution.py:52
  287.9 9.0 %attend2.1.refs_2_ = bf16[1024,128]{1,0:T(8,128)(2,1)S(1)} custom-call(s32[2]{0:T(128)S(1)} %pad_add_fusion.place, f32[1024,128]{1,0:T(8,128)S(1)} %get-tuple-element.73.mine, bf16[1024,128]{1,0:T(8,128)(2,1)S(1)} %collective-permute-done.30.other, bf16[1,128]{1,0:T(2,128)(2,1)S(1)} %get-tuple-element.132.bias, f32[1024,128]{1,0:T(8,128)S(1)} %get-tuple-element.137.cosine, ...), custom_call_target="tpu_custom_call" | custom-call | flops 4294967296 | bytes 2097152 | tf_op jit(solution)/shard_map/attend2/pallas_call | solution.py:52
  299.5 9.2 %attend3.1.refs_3_ = bf16[1024,128]{1,0:T(8,128)(2,1)S(1)} custom-call(s32[2]{0:T(128)S(1)} %pad_add_fusion.place, f32[1024,128]{1,0:T(8,128)S(1)} %get-tuple-element.81.mine, bf16[1024,128]{1,0:T(8,128)(2,1)S(1)} %collective-permute-done.36.other, bf16[1,128]{1,0:T(2,128)(2,1)S(1)} %get-tuple-element.131.bias, f32[1024,128]{1,0:T(8,128)S(1)} %get-tuple-element.137.cosine, ...), custom_call_target="tpu_custom_call" | custom-call | flops 4294967296 | bytes 2097152 | tf_op jit(solution)/shard_map/attend3/pallas_call | solution.py:52
  310.9 7.0 %collective-permute-done.42.refs_9_ = bf16[1024,128]{1,0:T(8,128)(2,1)S(1)} collective-permute-done((bf16[1024,128]{1,0:T(8,128)(2,1)S(1)}, bf16[1024,128]{1,0:T(8,128)(2,1)S(1)}, u32[]{:S(2)}, u32[]{:S(2)}) %collective-permute-start.42) | collective-permute-done | bytes 262176 | tf_op jit(solution)/shard_map/ppermute | solution.py:24
  317.9 5.6 %collective-permute-done.43.refs_10_ = bf16[1024,128]{1,0:T(8,128)(2,1)S(1)} collective-permute-done((bf16[1024,128]{1,0:T(8,128)(2,1)S(1)}, bf16[1024,128]{1,0:T(8,128)(2,1)S(1)}, u32[]{:S(2)}, u32[]{:S(2)}) %collective-permute-start.43) | collective-permute-done | bytes 262176 | tf_op jit(solution)/shard_map/ppermute | solution.py:24
  323.5 4.9 %collective-permute-done.44.refs_11_ = bf16[1024,128]{1,0:T(8,128)(2,1)S(1)} collective-permute-done((bf16[1024,128]{1,0:T(8,128)(2,1)S(1)}, bf16[1024,128]{1,0:T(8,128)(2,1)S(1)}, u32[]{:S(2)}, u32[]{:S(2)}) %collective-permute-start.44) | collective-permute-done | bytes 262176 | tf_op jit(solution)/shard_map/ppermute | solution.py:24
  331.1 3.8 collected.1.att
  334.9 6.9 %out_project0.1 = bf16[2,512,512]{2,1,0:T(8,128)(2,1)S(1)} custom-call(bf16[2,512,2048]{2,1,0:T(8,128)(2,1)} %collected.1.att, bf16[2048,128]{1,0:T(8,128)(2,1)} %get-tuple-element.83.refs_0_, bf16[2048,128]{1,0:T(8,128)(2,1)} %collective-permute-done.33.refs_1_, bf16[2048,128]{1,0:T(8,128)(2,1)S(1)} %collective-permute-done.49.refs_2_, ...), custom_call_target="tpu_custom_call" | custom-call | flops 2147483648 | bytes 7340032 | tf_op jit(solution)/shard_map/out_project0/pallas_call | solution.py:52
  342.5 6.7 %out_project1.1 = bf16[2,512,512]{2,1,0:T(8,128)(2,1)S(1)} custom-call(bf16[2,512,2048]{2,1,0:T(8,128)(2,1)} %collected.1.att, bf16[2048,128]{1,0:T(8,128)(2,1)S(1)} %copy-done.4, bf16[2048,128]{1,0:T(8,128)(2,1)S(1)} %collective-permute-done.52.refs_1_, bf16[2048,128]{1,0:T(8,128)(2,1)S(1)} %collective-permute-done.53.refs_2_, ...), custom_call_target="tpu_custom_call" | custom-call | flops 2147483648 | bytes 7340032 | tf_op jit(solution)/shard_map/out_project1/pallas_call | solution.py:52
  350.7 6.7 %out_project2.1 = bf16[2,512,512]{2,1,0:T(8,128)(2,1)S(1)} custom-call(bf16[2,512,2048]{2,1,0:T(8,128)(2,1)} %collected.1.att, bf16[2048,128]{1,0:T(8,128)(2,1)S(1)} %get-tuple-element.89.refs_0_, bf16[2048,128]{1,0:T(8,128)(2,1)S(1)} %collective-permute-done.56.refs_1_, bf16[2048,128]{1,0:T(8,128)(2,1)S(1)} %collective-permute-done.57.refs_2_, ...), custom_call_target="tpu_custom_call" | custom-call | flops 2147483648 | bytes 7340032 | tf_op jit(solution)/shard_map/out_project2/pallas_call | solution.py:52
  358.1 6.7 %out_project3.1 = bf16[2,512,512]{2,1,0:T(8,128)(2,1)S(1)} custom-call(bf16[2,512,2048]{2,1,0:T(8,128)(2,1)} %collected.1.att, bf16[2048,128]{1,0:T(8,128)(2,1)S(1)} %get-tuple-element.92.refs_0_, bf16[2048,128]{1,0:T(8,128)(2,1)S(1)} %collective-permute-done.60.refs_1_, bf16[2048,128]{1,0:T(8,128)(2,1)S(1)} %collective-permute-done.61.refs_2_, ...), custom_call_target="tpu_custom_call" | custom-call | flops 2147483648 | bytes 7340032 | tf_op jit(solution)/shard_map/out_project3/pallas_call | solution.py:52
  368.6 10.6 %collective-permute-done.59 = bf16[512,512]{1,0:T(8,128)(2,1)S(1)} collective-permute-done((bf16[512,512]{1,0:T(8,128)(2,1)S(1)}, bf16[512,512]{1,0:T(8,128)(2,1)S(1)}, u32[]{:S(2)}, u32[]{:S(2)}) %collective-permute-start.59) | collective-permute-done | bytes 524320 | tf_op jit(solution)/shard_map/ppermute | solution.py:29
  381.5 7.8 %collective-permute-done.63 = bf16[512,512]{1,0:T(8,128)(2,1)S(1)} collective-permute-done((bf16[512,512]{1,0:T(8,128)(2,1)S(1)}, bf16[512,512]{1,0:T(8,128)(2,1)S(1)}, u32[]{:S(2)}, u32[]{:S(2)}) %collective-permute-start.63) | collective-permute-done | bytes 524320 | tf_op jit(solution)/shard_map/ppermute | solution.py:29
  391.4 5.5 %collective-permute-done.67.refs_7_ = bf16[256,512]{1,0:T(8,128)(2,1)S(1)} collective-permute-done((bf16[256,512]{1,0:T(8,128)(2,1)S(1)}, bf16[256,512]{1,0:T(8,128)(2,1)S(1)}, u32[]{:S(2)}, u32[]{:S(2)}) %collective-permute-start.67) | collective-permute-done | bytes 262176 | tf_op jit(solution)/shard_map/ppermute | solution.py:24
  398.5 2.5 placed.1
  (271 shorter events, 77.9 us)
Async XLA Ops:
  6.6 15.0 %collective-permute-start.3 = (bf16[128,2048]{1,0:T(8,128)(2,1)S(1)}, bf16[128,2048]{1,0:T(8,128)(2,1)}, u32[]{:S(2)}, u32[]{:S(2)}) collective-permute-start(bf16[128,2048]{1,0:T(8,128)(2,1)S(1)} %get-tuple-element.107), channel_id=1, source_target_pairs={{0,8},{2,10},{4,12},{6,14},{8,0},{10,2},{12,4},{14,6},{16,24},{18,... | collective-permute-start | bytes 1572872 | tf_op jit(solution)/shard_map/ppermute | solution.py:24
  7.1 24.6 %collective-permute-start.1 = (bf16[128,2048]{1,0:T(8,128)(2,1)S(1)}, bf16[128,2048]{1,0:T(8,128)(2,1)}, u32[]{:S(2)}, u32[]{:S(2)}) collective-permute-start(bf16[128,2048]{1,0:T(8,128)(2,1)S(1)} %get-tuple-element.108), channel_id=1, source_target_pairs={{0,8},{2,10},{4,12},{6,14},{8,0},{10,2},{12,4},{14,6},{16,24},{18,... | collective-permute-start | bytes 1572872 | tf_op jit(solution)/shard_map/ppermute | solution.py:24
  33.1 24.8 %collective-permute-start.8 = (bf16[512,512]{1,0:T(8,128)(2,1)}, bf16[512,512]{1,0:T(8,128)(2,1)}, u32[]{:S(2)}, u32[]{:S(2)}) collective-permute-start(bf16[512,512]{1,0:T(8,128)(2,1)} %refs_0_.1), channel_id=1, source_target_pairs={{0,16},{2,18},{4,20},{6,22},{8,24},{10,26},{12,28},{14,30},{16,0},... | collective-permute-start | bytes 1572872 | tf_op jit(solution)/shard_map/ppermute | solution.py:24
  33.5 24.5 %collective-permute-start.9 = (bf16[512,512]{1,0:T(8,128)(2,1)}, bf16[512,512]{1,0:T(8,128)(2,1)}, u32[]{:S(2)}, u32[]{:S(2)}) collective-permute-start(bf16[512,512]{1,0:T(8,128)(2,1)} %refs_0_.1), channel_id=1, source_target_pairs={{0,4},{2,6},{4,0},{6,2},{8,12},{10,14},{12,8},{14,10},{16,20},{18,... | collective-permute-start | bytes 1572872 | tf_op jit(solution)/shard_map/ppermute | solution.py:24
  34.0 33.4 %collective-permute-start = (bf16[256,2048]{1,0:T(8,128)(2,1)S(1)}, bf16[256,2048]{1,0:T(8,128)(2,1)S(1)}, u32[]{:S(2)}, u32[]{:S(2)}) collective-permute-start(bf16[256,2048]{1,0:T(8,128)(2,1)S(1)} %get-tuple-element.49), channel_id=1, source_target_pairs={{0,2},{2,0},{4,6},{6,4},{8,10},{10,8},{12,14},{14,12},{16,18},{18,... | collective-permute-start | bytes 3145736 | tf_op jit(solution)/shard_map/ppermute | solution.py:24
  48.4 23.7 %collective-permute-start.5 = (bf16[256,2048]{1,0:T(8,128)(2,1)}, bf16[256,2048]{1,0:T(8,128)(2,1)}, u32[]{:S(2)}, u32[]{:S(2)}) collective-permute-start(bf16[256,2048]{1,0:T(8,128)(2,1)} %pad_maximum_fusion.1), channel_id=1, source_target_pairs={{0,2},{2,0},{4,6},{6,4},{8,10},{10,8},{12,14},{14,12},{16,18},{18,... | collective-permute-start | bytes 3145736 | tf_op jit(solution)/shard_map/ppermute | solution.py:24
  80.2 14.4 %collective-permute-start.6 = (bf16[512,512]{1,0:T(8,128)(2,1)S(1)}, bf16[512,512]{1,0:T(8,128)(2,1)S(1)}, u32[]{:S(2)}, u32[]{:S(2)}) collective-permute-start(bf16[512,512]{1,0:T(8,128)(2,1)S(1)} %reshape_squeeze.12.refs_0_), channel_id=1, source_target_pairs={{0,4},{2,6},{4,0},{6,2},{8,12},{10,14},{12,8},{14,10},{16,20},{18,... | collective-permute-start | bytes 1572872 | tf_op jit(solution)/shard_map/ppermute | solution.py:24
  80.7 34.1 %collective-permute-start.7 = (bf16[512,512]{1,0:T(8,128)(2,1)S(1)}, bf16[512,512]{1,0:T(8,128)(2,1)S(1)}, u32[]{:S(2)}, u32[]{:S(2)}) collective-permute-start(bf16[512,512]{1,0:T(8,128)(2,1)S(1)} %reshape_squeeze.12.refs_0_), channel_id=1, source_target_pairs={{0,16},{2,18},{4,20},{6,22},{8,24},{10,26},{12,28},{14,30},{16,0},... | collective-permute-start | bytes 1572872 | tf_op jit(solution)/shard_map/ppermute | solution.py:24
  83.4 32.9 %collective-permute-start.15 = (bf16[256,512]{1,0:T(8,128)(2,1)S(1)}, bf16[256,512]{1,0:T(8,128)(2,1)S(1)}, u32[]{:S(2)}, u32[]{:S(2)}) collective-permute-start(bf16[256,512]{1,0:T(8,128)(2,1)S(1)} %slice.313), channel_id=1, source_target_pairs={{0,8},{2,10},{4,12},{6,14},{8,0},{10,2},{12,4},{14,6},{16,24},{18,... | collective-permute-start | bytes 786440 | tf_op jit(solution)/shard_map/ppermute | solution.py:24
  85.5 51.9 %collective-permute-start.18 = (bf16[512,512]{1,0:T(8,128)(2,1)S(1)}, bf16[512,512]{1,0:T(8,128)(2,1)}, u32[]{:S(2)}, u32[]{:S(2)}) collective-permute-start(bf16[512,512]{1,0:T(8,128)(2,1)S(1)} %reshape_squeeze.13.refs_0_), channel_id=1, source_target_pairs={{0,16},{2,18},{4,20},{6,22},{8,24},{10,26},{12,28},{14,30},{16,0},... | collective-permute-start | bytes 1572872 | tf_op jit(solution)/shard_map/ppermute | solution.py:24
  94.5 25.2 %collective-permute-start.25 = (bf16[512,512]{1,0:T(8,128)(2,1)S(1)}, bf16[512,512]{1,0:T(8,128)(2,1)S(1)}, u32[]{:S(2)}, u32[]{:S(2)}) collective-permute-start(bf16[512,512]{1,0:T(8,128)(2,1)S(1)} %reshape_squeeze.13.refs_0_), channel_id=1, source_target_pairs={{0,4},{2,6},{4,0},{6,2},{8,12},{10,14},{12,8},{14,10},{16,20},{18,... | collective-permute-start | bytes 1572872 | tf_op jit(solution)/shard_map/ppermute | solution.py:24
  114.8 22.6 %collective-permute-start.11 = (bf16[512,512]{1,0:T(8,128)(2,1)S(1)}, bf16[512,512]{1,0:T(8,128)(2,1)}, u32[]{:S(2)}, u32[]{:S(2)}) collective-permute-start(bf16[512,512]{1,0:T(8,128)(2,1)S(1)} %collective-permute-done.7.refs_2_), channel_id=1, source_target_pairs={{0,4},{2,6},{4,0},{6,2},{8,12},{10,14},{12,8},{14,10},{16,20},{18,... | collective-permute-start | bytes 1572872 | tf_op jit(solution)/shard_map/ppermute | solution.py:24
  117.8 21.1 %collective-permute-start.16 = (bf16[256,512]{1,0:T(8,128)(2,1)}, bf16[256,512]{1,0:T(8,128)(2,1)}, u32[]{:S(2)}, u32[]{:S(2)}) collective-permute-start(bf16[256,512]{1,0:T(8,128)(2,1)} %pad_maximum_fusion.7), channel_id=1, source_target_pairs={{0,1},{1,0},{2,3},{3,2},{4,5},{5,4},{6,7},{7,6},{8,9},{9,8},{10,11... | collective-permute-start | bytes 786440 | tf_op jit(solution)/shard_map/ppermute | solution.py:29
  119.6 29.0 %collective-permute-start.20 = (bf16[512,512]{1,0:T(8,128)(2,1)S(1)}, bf16[512,512]{1,0:T(8,128)(2,1)}, u32[]{:S(2)}, u32[]{:S(2)}) collective-permute-start(bf16[512,512]{1,0:T(8,128)(2,1)S(1)} %reshape_squeeze.14.refs_0_), channel_id=1, source_target_pairs={{0,16},{2,18},{4,20},{6,22},{8,24},{10,26},{12,28},{14,30},{16,0},... | collective-permute-start | bytes 1572872 | tf_op jit(solution)/shard_map/ppermute | solution.py:24
  119.7 23.4 %collective-permute-start.28 = (bf16[512,512]{1,0:T(8,128)(2,1)S(1)}, bf16[512,512]{1,0:T(8,128)(2,1)S(1)}, u32[]{:S(2)}, u32[]{:S(2)}) collective-permute-start(bf16[512,512]{1,0:T(8,128)(2,1)S(1)} %reshape_squeeze.14.refs_0_), channel_id=1, source_target_pairs={{0,4},{2,6},{4,0},{6,2},{8,12},{10,14},{12,8},{14,10},{16,20},{18,... | collective-permute-start | bytes 1572872 | tf_op jit(solution)/shard_map/ppermute | solution.py:24
  137.4 15.0 %collective-permute-start.21 = (bf16[512,512]{1,0:T(8,128)(2,1)}, bf16[512,512]{1,0:T(8,128)(2,1)S(1)}, u32[]{:S(2)}, u32[]{:S(2)}) collective-permute-start(bf16[512,512]{1,0:T(8,128)(2,1)} %collective-permute-done.18.refs_2_), channel_id=1, source_target_pairs={{0,4},{2,6},{4,0},{6,2},{8,12},{10,14},{12,8},{14,10},{16,20},{18,... | collective-permute-start | bytes 1572872 | tf_op jit(solution)/shard_map/ppermute | solution.py:24
  143.1 20.5 %collective-permute-start.31 = (bf16[512,512]{1,0:T(8,128)(2,1)S(1)}, bf16[512,512]{1,0:T(8,128)(2,1)S(1)}, u32[]{:S(2)}, u32[]{:S(2)}) collective-permute-start(bf16[512,512]{1,0:T(8,128)(2,1)S(1)} %reshape_squeeze.15.refs_0_), channel_id=1, source_target_pairs={{0,4},{2,6},{4,0},{6,2},{8,12},{10,14},{12,8},{14,10},{16,20},{18,... | collective-permute-start | bytes 1572872 | tf_op jit(solution)/shard_map/ppermute | solution.py:24
  153.2 27.6 %collective-permute-start.22 = (bf16[512,512]{1,0:T(8,128)(2,1)}, bf16[512,512]{1,0:T(8,128)(2,1)S(1)}, u32[]{:S(2)}, u32[]{:S(2)}) collective-permute-start(bf16[512,512]{1,0:T(8,128)(2,1)} %collective-permute-done.20.refs_2_), channel_id=1, source_target_pairs={{0,4},{2,6},{4,0},{6,2},{8,12},{10,14},{12,8},{14,10},{16,20},{18,... | collective-permute-start | bytes 1572872 | tf_op jit(solution)/shard_map/ppermute | solution.py:24
  155.7 24.3 %collective-permute-start.19 = (bf16[512,256]{1,0:T(8,128)(2,1)S(1)}, bf16[512,256]{1,0:T(8,128)(2,1)S(1)}, u32[]{:S(2)}, u32[]{:S(2)}) collective-permute-start(bf16[512,256]{1,0:T(8,128)(2,1)S(1)} %pad_maximum_fusion.8), channel_id=1, source_target_pairs={{0,16},{2,18},{4,20},{6,22},{8,24},{10,26},{12,28},{14,30},{16,0},... | collective-permute-start | bytes 786440 | tf_op jit(solution)/shard_map/ppermute | solution.py:24
  158.5 44.0 %collective-permute-start.32 = (bf16[512,512]{1,0:T(8,128)(2,1)S(1)}, bf16[512,512]{1,0:T(8,128)(2,1)}, u32[]{:S(2)}, u32[]{:S(2)}) collective-permute-start(bf16[512,512]{1,0:T(8,128)(2,1)S(1)} %reshape_squeeze.15.refs_0_), channel_id=1, source_target_pairs={{0,16},{2,18},{4,20},{6,22},{8,24},{10,26},{12,28},{14,30},{16,0},... | collective-permute-start | bytes 1572872 | tf_op jit(solution)/shard_map/ppermute | solution.py:24
  164.4 38.0 %collective-permute-start.33 = (bf16[2048,128]{1,0:T(8,128)(2,1)}, bf16[2048,128]{1,0:T(8,128)(2,1)}, u32[]{:S(2)}, u32[]{:S(2)}) collective-permute-start(bf16[2048,128]{1,0:T(8,128)(2,1)} %get-tuple-element.83.refs_0_), channel_id=1, source_target_pairs={{0,4},{2,6},{4,0},{6,2},{8,12},{10,14},{12,8},{14,10},{16,20},{18,... | collective-permute-start | bytes 1572872 | tf_op jit(solution)/shard_map/ppermute | solution.py:24
  181.6 21.4 %collective-permute-start.23 = (bf16[1024,256]{1,0:T(8,128)(2,1)}, bf16[1024,256]{1,0:T(8,128)(2,1)}, u32[]{:S(2)}, u32[]{:S(2)}) collective-permute-start(bf16[1024,256]{1,0:T(8,128)(2,1)} %pad_maximum_fusion.4), channel_id=1, source_target_pairs={{0,4},{2,6},{4,0},{6,2},{8,12},{10,14},{12,8},{14,10},{16,20},{18,... | collective-permute-start | bytes 1572872 | tf_op jit(solution)/shard_map/ppermute | solution.py:24
  182.1 30.9 %collective-permute-start.49 = (bf16[2048,128]{1,0:T(8,128)(2,1)}, bf16[2048,128]{1,0:T(8,128)(2,1)S(1)}, u32[]{:S(2)}, u32[]{:S(2)}) collective-permute-start(bf16[2048,128]{1,0:T(8,128)(2,1)} %get-tuple-element.83.refs_0_), channel_id=1, source_target_pairs={{0,16},{2,18},{4,20},{6,22},{8,24},{10,26},{12,28},{14,30},{16,0},... | collective-permute-start | bytes 1572872 | tf_op jit(solution)/shard_map/ppermute | solution.py:24
  190.9 47.4 %collective-permute-start.12 = (bf16[1024,256]{1,0:T(8,128)(2,1)S(1)}, bf16[1024,256]{1,0:T(8,128)(2,1)S(1)}, u32[]{:S(2)}, u32[]{:S(2)}) collective-permute-start(bf16[1024,256]{1,0:T(8,128)(2,1)S(1)} %get-tuple-element.54), channel_id=1, source_target_pairs={{0,2},{2,0},{4,6},{6,4},{8,10},{10,8},{12,14},{14,12},{16,18},{18,... | collective-permute-start | bytes 1572872 | tf_op jit(solution)/shard_map/ppermute | solution.py:24
  202.5 15.1 %collective-permute-start.34 = (bf16[512,512]{1,0:T(8,128)(2,1)}, bf16[512,512]{1,0:T(8,128)(2,1)S(1)}, u32[]{:S(2)}, u32[]{:S(2)}) collective-permute-start(bf16[512,512]{1,0:T(8,128)(2,1)} %collective-permute-done.32.refs_2_), channel_id=1, source_target_pairs={{0,4},{2,6},{4,0},{6,2},{8,12},{10,14},{12,8},{14,10},{16,20},{18,... | collective-permute-start | bytes 1572872 | tf_op jit(solution)/shard_map/ppermute | solution.py:24
  203.0 22.3 %collective-permute-start.52 = (bf16[2048,128]{1,0:T(8,128)(2,1)S(1)}, bf16[2048,128]{1,0:T(8,128)(2,1)S(1)}, u32[]{:S(2)}, u32[]{:S(2)}) collective-permute-start(bf16[2048,128]{1,0:T(8,128)(2,1)S(1)} %copy-done.4), channel_id=1, source_target_pairs={{0,4},{2,6},{4,0},{6,2},{8,12},{10,14},{12,8},{14,10},{16,20},{18,... | collective-permute-start | bytes 1572872 | tf_op jit(solution)/shard_map/ppermute | solution.py:24
  208.7 30.4 %collective-permute-start.26 = (bf16[1024,256]{1,0:T(8,128)(2,1)S(1)}, bf16[1024,256]{1,0:T(8,128)(2,1)S(1)}, u32[]{:S(2)}, u32[]{:S(2)}) collective-permute-start(bf16[1024,256]{1,0:T(8,128)(2,1)S(1)} %get-tuple-element.67), channel_id=1, source_target_pairs={{0,2},{2,0},{4,6},{6,4},{8,10},{10,8},{12,14},{14,12},{16,18},{18,... | collective-permute-start | bytes 1572872 | tf_op jit(solution)/shard_map/ppermute | solution.py:24
  213.0 25.2 %collective-permute-start.53 = (bf16[2048,128]{1,0:T(8,128)(2,1)S(1)}, bf16[2048,128]{1,0:T(8,128)(2,1)S(1)}, u32[]{:S(2)}, u32[]{:S(2)}) collective-permute-start(bf16[2048,128]{1,0:T(8,128)(2,1)S(1)} %copy-done.4), channel_id=1, source_target_pairs={{0,16},{2,18},{4,20},{6,22},{8,24},{10,26},{12,28},{14,30},{16,0},... | collective-permute-start | bytes 1572872 | tf_op jit(solution)/shard_map/ppermute | solution.py:24
  217.6 22.8 %collective-permute-start.29 = (bf16[1024,256]{1,0:T(8,128)(2,1)S(1)}, bf16[1024,256]{1,0:T(8,128)(2,1)S(1)}, u32[]{:S(2)}, u32[]{:S(2)}) collective-permute-start(bf16[1024,256]{1,0:T(8,128)(2,1)S(1)} %get-tuple-element.72), channel_id=1, source_target_pairs={{0,2},{2,0},{4,6},{6,4},{8,10},{10,8},{12,14},{14,12},{16,18},{18,... | collective-permute-start | bytes 1572872 | tf_op jit(solution)/shard_map/ppermute | solution.py:24
  225.3 41.0 %collective-permute-start.24 = (bf16[2048,256]{1,0:T(8,128)(2,1)}, bf16[2048,256]{1,0:T(8,128)(2,1)}, u32[]{:S(2)}, u32[]{:S(2)}) collective-permute-start(bf16[2048,256]{1,0:T(8,128)(2,1)} %pad_maximum_fusion.2), channel_id=1, source_target_pairs={{0,2},{2,0},{4,6},{6,4},{8,10},{10,8},{12,14},{14,12},{16,18},{18,... | collective-permute-start | bytes 3145736 | tf_op jit(solution)/shard_map/ppermute | solution.py:24
  238.2 14.8 %collective-permute-start.50 = (bf16[2048,128]{1,0:T(8,128)(2,1)S(1)}, bf16[2048,128]{1,0:T(8,128)(2,1)S(1)}, u32[]{:S(2)}, u32[]{:S(2)}) collective-permute-start(bf16[2048,128]{1,0:T(8,128)(2,1)S(1)} %collective-permute-done.49.refs_2_), channel_id=1, source_target_pairs={{0,4},{2,6},{4,0},{6,2},{8,12},{10,14},{12,8},{14,10},{16,20},{18,... | collective-permute-start | bytes 1572872 | tf_op jit(solution)/shard_map/ppermute | solution.py:24
  239.1 24.7 %collective-permute-start.56 = (bf16[2048,128]{1,0:T(8,128)(2,1)S(1)}, bf16[2048,128]{1,0:T(8,128)(2,1)S(1)}, u32[]{:S(2)}, u32[]{:S(2)}) collective-permute-start(bf16[2048,128]{1,0:T(8,128)(2,1)S(1)} %get-tuple-element.89.refs_0_), channel_id=1, source_target_pairs={{0,4},{2,6},{4,0},{6,2},{8,12},{10,14},{12,8},{14,10},{16,20},{18,... | collective-permute-start | bytes 1572872 | tf_op jit(solution)/shard_map/ppermute | solution.py:24
  240.3 25.9 %collective-permute-start.57 = (bf16[2048,128]{1,0:T(8,128)(2,1)S(1)}, bf16[2048,128]{1,0:T(8,128)(2,1)S(1)}, u32[]{:S(2)}, u32[]{:S(2)}) collective-permute-start(bf16[2048,128]{1,0:T(8,128)(2,1)S(1)} %get-tuple-element.89.refs_0_), channel_id=1, source_target_pairs={{0,16},{2,18},{4,20},{6,22},{8,24},{10,26},{12,28},{14,30},{16,0},... | collective-permute-start | bytes 1572872 | tf_op jit(solution)/shard_map/ppermute | solution.py:24
  244.3 24.0 %collective-permute-start.13 = (bf16[1024,128]{1,0:T(8,128)(2,1)S(1)}, bf16[1024,128]{1,0:T(8,128)(2,1)S(1)}, u32[]{:S(2)}, u32[]{:S(2)}) collective-permute-start(bf16[1024,128]{1,0:T(8,128)(2,1)S(1)} %get-tuple-element.56), channel_id=1, source_target_pairs={{0,8},{2,10},{4,12},{6,14},{8,0},{10,2},{12,4},{14,6},{16,24},{18,... | collective-permute-start | bytes 786440 | tf_op jit(solution)/shard_map/ppermute | solution.py:24
  253.0 25.7 %collective-permute-start.27 = (bf16[1024,128]{1,0:T(8,128)(2,1)S(1)}, bf16[1024,128]{1,0:T(8,128)(2,1)S(1)}, u32[]{:S(2)}, u32[]{:S(2)}) collective-permute-start(bf16[1024,128]{1,0:T(8,128)(2,1)S(1)} %get-tuple-element.69), channel_id=1, source_target_pairs={{0,8},{2,10},{4,12},{6,14},{8,0},{10,2},{12,4},{14,6},{16,24},{18,... | collective-permute-start | bytes 786440 | tf_op jit(solution)/shard_map/ppermute | solution.py:24
  263.8 24.0 %collective-permute-start.30 = (bf16[1024,128]{1,0:T(8,128)(2,1)S(1)}, bf16[1024,128]{1,0:T(8,128)(2,1)S(1)}, u32[]{:S(2)}, u32[]{:S(2)}) collective-permute-start(bf16[1024,128]{1,0:T(8,128)(2,1)S(1)} %get-tuple-element.74), channel_id=1, source_target_pairs={{0,8},{2,10},{4,12},{6,14},{8,0},{10,2},{12,4},{14,6},{16,24},{18,... | collective-permute-start | bytes 786440 | tf_op jit(solution)/shard_map/ppermute | solution.py:24
  266.3 30.6 %collective-permute-start.36 = (bf16[1024,128]{1,0:T(8,128)(2,1)S(1)}, bf16[1024,128]{1,0:T(8,128)(2,1)S(1)}, u32[]{:S(2)}, u32[]{:S(2)}) collective-permute-start(bf16[1024,128]{1,0:T(8,128)(2,1)S(1)} %get-tuple-element.82), channel_id=1, source_target_pairs={{0,8},{2,10},{4,12},{6,14},{8,0},{10,2},{12,4},{14,6},{16,24},{18,... | collective-permute-start | bytes 786440 | tf_op jit(solution)/shard_map/ppermute | solution.py:24
  266.3 32.7 %collective-permute-start.54 = (bf16[2048,128]{1,0:T(8,128)(2,1)S(1)}, bf16[2048,128]{1,0:T(8,128)(2,1)S(1)}, u32[]{:S(2)}, u32[]{:S(2)}) collective-permute-start(bf16[2048,128]{1,0:T(8,128)(2,1)S(1)} %collective-permute-done.53.refs_2_), channel_id=1, source_target_pairs={{0,4},{2,6},{4,0},{6,2},{8,12},{10,14},{12,8},{14,10},{16,20},{18,... | collective-permute-start | bytes 1572872 | tf_op jit(solution)/shard_map/ppermute | solution.py:24
  268.4 60.1 %collective-permute-start.60 = (bf16[2048,128]{1,0:T(8,128)(2,1)S(1)}, bf16[2048,128]{1,0:T(8,128)(2,1)S(1)}, u32[]{:S(2)}, u32[]{:S(2)}) collective-permute-start(bf16[2048,128]{1,0:T(8,128)(2,1)S(1)} %get-tuple-element.92.refs_0_), channel_id=1, source_target_pairs={{0,4},{2,6},{4,0},{6,2},{8,12},{10,14},{12,8},{14,10},{16,20},{18,... | collective-permute-start | bytes 1572872 | tf_op jit(solution)/shard_map/ppermute | solution.py:24
  278.7 50.2 %collective-permute-start.61 = (bf16[2048,128]{1,0:T(8,128)(2,1)S(1)}, bf16[2048,128]{1,0:T(8,128)(2,1)S(1)}, u32[]{:S(2)}, u32[]{:S(2)}) collective-permute-start(bf16[2048,128]{1,0:T(8,128)(2,1)S(1)} %get-tuple-element.92.refs_0_), channel_id=1, source_target_pairs={{0,16},{2,18},{4,20},{6,22},{8,24},{10,26},{12,28},{14,30},{16,0},... | collective-permute-start | bytes 1572872 | tf_op jit(solution)/shard_map/ppermute | solution.py:24
  308.9 14.6 %collective-permute-start.43 = (bf16[1024,128]{1,0:T(8,128)(2,1)S(1)}, bf16[1024,128]{1,0:T(8,128)(2,1)S(1)}, u32[]{:S(2)}, u32[]{:S(2)}) collective-permute-start(bf16[1024,128]{1,0:T(8,128)(2,1)S(1)} %attend2.1.refs_2_), channel_id=1, source_target_pairs={{0,8},{2,10},{4,12},{6,14},{8,0},{10,2},{12,4},{14,6},{16,24},{18,... | collective-permute-start | bytes 786440 | tf_op jit(solution)/shard_map/ppermute | solution.py:24
  310.8 17.6 %collective-permute-start.44 = (bf16[1024,128]{1,0:T(8,128)(2,1)S(1)}, bf16[1024,128]{1,0:T(8,128)(2,1)S(1)}, u32[]{:S(2)}, u32[]{:S(2)}) collective-permute-start(bf16[1024,128]{1,0:T(8,128)(2,1)S(1)} %attend3.1.refs_3_), channel_id=1, source_target_pairs={{0,8},{2,10},{4,12},{6,14},{8,0},{10,2},{12,4},{14,6},{16,24},{18,... | collective-permute-start | bytes 786440 | tf_op jit(solution)/shard_map/ppermute | solution.py:24
  329.0 21.7 %collective-permute-start.58 = (bf16[2048,128]{1,0:T(8,128)(2,1)S(1)}, bf16[2048,128]{1,0:T(8,128)(2,1)S(1)}, u32[]{:S(2)}, u32[]{:S(2)}) collective-permute-start(bf16[2048,128]{1,0:T(8,128)(2,1)S(1)} %collective-permute-done.57.refs_2_), channel_id=1, source_target_pairs={{0,4},{2,6},{4,0},{6,2},{8,12},{10,14},{12,8},{14,10},{16,20},{18,... | collective-permute-start | bytes 1572872 | tf_op jit(solution)/shard_map/ppermute | solution.py:24
  329.0 29.0 %collective-permute-start.62 = (bf16[2048,128]{1,0:T(8,128)(2,1)S(1)}, bf16[2048,128]{1,0:T(8,128)(2,1)S(1)}, u32[]{:S(2)}, u32[]{:S(2)}) collective-permute-start(bf16[2048,128]{1,0:T(8,128)(2,1)S(1)} %collective-permute-done.61.refs_2_), channel_id=1, source_target_pairs={{0,4},{2,6},{4,0},{6,2},{8,12},{10,14},{12,8},{14,10},{16,20},{18,... | collective-permute-start | bytes 1572872 | tf_op jit(solution)/shard_map/ppermute | solution.py:24
  341.9 24.5 %collective-permute-start.51 = (bf16[512,512]{1,0:T(8,128)(2,1)S(1)}, bf16[512,512]{1,0:T(8,128)(2,1)S(1)}, u32[]{:S(2)}, u32[]{:S(2)}) collective-permute-start(bf16[512,512]{1,0:T(8,128)(2,1)S(1)} %slice_bitcast_fusion.6), channel_id=1, source_target_pairs={{0,1},{1,0},{2,3},{3,2},{4,5},{5,4},{6,7},{7,6},{8,9},{9,8},{10,11... | collective-permute-start | bytes 1572872 | tf_op jit(solution)/shard_map/ppermute | solution.py:29
  349.2 18.8 %collective-permute-start.55 = (bf16[512,512]{1,0:T(8,128)(2,1)S(1)}, bf16[512,512]{1,0:T(8,128)(2,1)S(1)}, u32[]{:S(2)}, u32[]{:S(2)}) collective-permute-start(bf16[512,512]{1,0:T(8,128)(2,1)S(1)} %slice_bitcast_fusion.4), channel_id=1, source_target_pairs={{0,1},{1,0},{2,3},{3,2},{4,5},{5,4},{6,7},{7,6},{8,9},{9,8},{10,11... | collective-permute-start | bytes 1572872 | tf_op jit(solution)/shard_map/ppermute | solution.py:29
  357.5 21.7 %collective-permute-start.59 = (bf16[512,512]{1,0:T(8,128)(2,1)S(1)}, bf16[512,512]{1,0:T(8,128)(2,1)S(1)}, u32[]{:S(2)}, u32[]{:S(2)}) collective-permute-start(bf16[512,512]{1,0:T(8,128)(2,1)S(1)} %slice_bitcast_fusion.2), channel_id=1, source_target_pairs={{0,1},{1,0},{2,3},{3,2},{4,5},{5,4},{6,7},{7,6},{8,9},{9,8},{10,11... | collective-permute-start | bytes 1572872 | tf_op jit(solution)/shard_map/ppermute | solution.py:29
  364.8 24.5 %collective-permute-start.63 = (bf16[512,512]{1,0:T(8,128)(2,1)S(1)}, bf16[512,512]{1,0:T(8,128)(2,1)S(1)}, u32[]{:S(2)}, u32[]{:S(2)}) collective-permute-start(bf16[512,512]{1,0:T(8,128)(2,1)S(1)} %slice_bitcast_fusion), channel_id=1, source_target_pairs={{0,1},{1,0},{2,3},{3,2},{4,5},{5,4},{6,7},{7,6},{8,9},{9,8},{10,11... | collective-permute-start | bytes 1572872 | tf_op jit(solution)/shard_map/ppermute | solution.py:29
  (69 other events, 945.6 us)
